TPU v7x, 512 devices: a whole 4x8x8 slice. The times are simulated.
512 devices in a mesh: row: 32 (over x, z_hi, core), col: 16 (over y, z_lo).
Axes of the slice: x: 4, y: 8, z: 8 (z_hi: 4, z_lo: 2; z = z_hi * 2 + z_lo), core: 2. Of those that a mesh axis runs over, the one named last changes fastest.
Arguments:
- pair_tensor: bfloat16 [512, 512, 128], P('row', 'col'), may hold values from -6 to 6
- ln_gain: bfloat16 [128], replicated, may hold values from 0.099609375 to 1.8984375
- query_weight: bfloat16 [128, 128], replicated, may hold values from -1.3203125 to 1.3203125
- key_weight: bfloat16 [128, 128], replicated, may hold values from -0.5 to 0.5
- value_weight: bfloat16 [128, 128], replicated, may hold values from -0.5 to 0.5
- gate_weight: bfloat16 [128, 128], replicated, may hold values from -0.5 to 0.5
- bias_weight: bfloat16 [128, 4], replicated, may hold values from -42.426407 to 42.426407
- out_weight: bfloat16 [128, 128], replicated, may hold values from -2.109375 to 2.109375
Outputs:
- update: bfloat16 [512, 512, 128], P('row', 'col')
- update_mirror: bfloat16 [512, 512, 128], P('row', 'col')
All inputs are finite; a program needn't handle non-finite values.
Results may differ from a plain program's by a relative error of at most 0.008.
The roundings to bfloat16 on the way count: a program that leaves them out, or rounds other values in their place, can miss the bound.
Values may be sent and summed in bfloat16 or wider, within the bound.
A program may use at most 64 MiB of HBM per device.

v0:
```python
import math

import jax
import jax.numpy as jnp
from jax import lax
from jax.sharding import PartitionSpec as P

EPSILON = 1e-05


def partner(block, axis, distance):
    count = lax.axis_size(axis)
    route = []
    for low in range(count):
        high = low | 1 << distance
        if high != low and high < count:
            route += [(low, high), (high, low)]
    return lax.ppermute(block, axis, route)


def normalize(pair_tensor, ln_gain):
    entries = pair_tensor.astype(jnp.float32)
    center = jnp.mean(entries, axis=-1, keepdims=True)
    spread = jnp.mean(jnp.square(entries - center), axis=-1, keepdims=True)
    return ((entries - center) * lax.rsqrt(spread + EPSILON) * ln_gain.astype(jnp.float32)).astype(
        jnp.bfloat16
    )


def project(flat_rows, weight):
    return jnp.dot(flat_rows, weight, preferred_element_type=jnp.float32)


def mirror_butterfly(matrix):
    half_width = matrix.shape[1] // 2
    on_even = lax.axis_index("row") % 2 == 0
    first_half = matrix[:, :half_width]
    second_half = matrix[:, half_width:]
    outgoing = jnp.where(on_even, second_half, first_half)
    kept_half = jnp.where(on_even, first_half, second_half)
    arrived = partner(outgoing, "row", 0)
    joined = jnp.where(
        on_even, jnp.concatenate([kept_half, arrived], 0), jnp.concatenate([arrived, kept_half], 0)
    )
    row_group = lax.axis_index("row") // 2
    column = lax.axis_index("col")
    for bit_level in range(lax.axis_size("col").bit_length() - 1):
        across = partner(joined, "row", bit_level + 1)
        across = partner(across, "col", bit_level)
        differs = row_group // 2**bit_level % 2 != column // 2**bit_level % 2
        joined = jnp.where(differs, across, joined)
    return joined


def mirror(matrix):
    return mirror_butterfly(matrix)


def online_step(running, queries, key_part, value_part, bias_part):
    running_max, denominator, weighted = running
    scores = jnp.einsum("ijhd,ikhd->ihjk", queries, key_part, preferred_element_type=jnp.float32)
    scores = scores + bias_part[None].astype(jnp.float32)
    new_max = jnp.maximum(running_max, jnp.max(scores, axis=-1))
    factor = jnp.exp(running_max - new_max)
    exponent = jnp.exp(scores - new_max[..., None])
    denominator = denominator * factor + jnp.sum(exponent, axis=-1)
    weights = exponent.astype(jnp.bfloat16)
    weighted = weighted * factor[..., None] + jnp.einsum(
        "ihjk,ikhd->ihjd", weights, value_part, preferred_element_type=jnp.float32
    )
    return (new_max, denominator, weighted)


def fold_blocks(running, queries, source, bias_rows, make_pair):
    key_count = source[0].shape[1]
    block_size = math.gcd(key_count, 128)
    block_total = key_count // block_size
    row_count = source[0].shape[0]
    stacked = tuple(
        (
            jnp.moveaxis(member.reshape(row_count, block_total, block_size, member.shape[2]), 1, 0)
            for member in source
        )
    )
    bias_stack = jnp.moveaxis(
        bias_rows.reshape(bias_rows.shape[0], bias_rows.shape[1], block_total, block_size), 2, 0
    )

    def one_block(current, inputs):
        pieces, bias_block = inputs
        key_part, value_part = make_pair(pieces)
        return (online_step(current, queries, key_part, value_part, bias_block), None)

    running, unused = lax.scan(one_block, running, (stacked, bias_stack))
    return running


def per_device(
    pair_tensor,
    ln_gain,
    query_weight,
    key_weight,
    value_weight,
    gate_weight,
    bias_weight,
    out_weight,
):
    rows_here, cols_here, channels = pair_tensor.shape
    head_count = bias_weight.shape[1]
    head_dim = channels // head_count
    score_scale = head_dim ** (-0.5)
    normed = normalize(pair_tensor, ln_gain)
    flat_rows = normed.reshape(-1, channels)
    bias_tile = (
        project(flat_rows, bias_weight)
        .astype(jnp.bfloat16)
        .reshape(rows_here, cols_here * head_count)
    )
    queries = (
        (project(flat_rows, query_weight) * score_scale)
        .astype(jnp.bfloat16)
        .reshape(rows_here, cols_here, head_count, head_dim)
    )
    gating = jax.nn.sigmoid(project(flat_rows, gate_weight)).reshape(rows_here, cols_here, channels)
    mirrored = mirror(bias_tile)
    bias_rows = lax.all_gather(mirrored, "row", axis=1, tiled=True)
    bias_rows = bias_rows.reshape(cols_here, -1, head_count).transpose(2, 0, 1)
    start_state = (
        jnp.full((rows_here, head_count, cols_here), -1e30, jnp.float32),
        jnp.zeros((rows_here, head_count, cols_here), jnp.float32),
        jnp.zeros((rows_here, head_count, cols_here, head_dim), jnp.float32),
    )

    def from_normed(pieces):
        block_rows = pieces[0]
        shape_out = block_rows.shape[:2] + (head_count, head_dim)
        flat_block = block_rows.reshape(-1, channels)
        key_part = project(flat_block, key_weight).astype(jnp.bfloat16).reshape(shape_out)
        value_part = project(flat_block, value_weight).astype(jnp.bfloat16).reshape(shape_out)
        return (key_part, value_part)

    final_state = fold_blocks(
        start_state,
        queries,
        (lax.all_gather(normed, "col", axis=1, tiled=True),),
        bias_rows,
        from_normed,
    )
    unused_max, denominator, weighted = final_state
    attended = (
        (weighted / denominator[..., None])
        .transpose(0, 2, 1, 3)
        .reshape(rows_here, cols_here, channels)
    )
    gated = (gating * attended).astype(jnp.bfloat16)
    update = (
        project(gated.reshape(-1, channels), out_weight)
        .astype(jnp.bfloat16)
        .reshape(rows_here, cols_here, channels)
    )
    mirrored_update = mirror(update.reshape(rows_here, cols_here * channels))
    update_mirror = jnp.swapaxes(mirrored_update.reshape(cols_here, rows_here, channels), 0, 1)
    return (update, update_mirror)


def solution(mesh):
    placed = (P("row", "col", None), P(), P(), P(), P(), P(), P(), P())
    return jax.shard_map(
        per_device,
        mesh=mesh,
        in_specs=placed,
        out_specs=(P("row", "col", None), P("row", "col", None)),
        check_vma=False,
    )
```

profile of v0, /device:TPU:56, one launch (start us, length us, event | category | flops | bytes accessed | tf_op | source)
XLA Modules:
  0.0 229.2 jit_solution(50999845978497473)
XLA Ops:
  13.4 1.9 collective-permute-start
  16.5 6.1 %collective-permute-start.1 = (bf16[32,64]{1,0:T(8,128)(2,1)S(1)}, bf16[32,64]{1,0:T(8,128)(2,1)S(1)}, u32[]{:S(2)}, u32[]{:S(2)}) collective-permute-start(bf16[32,64]{1,0:T(8,128)(2,1)S(1)} %maximum_select_fusion.1), channel_id=1, source_target_pairs={{0,32},{32,0},{16,48},{48,16},{64,96},{96,64},{80,112},{112,80},{1... | collective-permute-start | bytes 12296 | tf_op jit(solution)/shard_map/ppermute | solution.py:18
  24.2 4.3 %collective-permute-start.2 = (bf16[32,64]{1,0:T(8,128)(2,1)S(1)}, bf16[32,64]{1,0:T(8,128)(2,1)S(1)}, u32[]{:S(2)}, u32[]{:S(2)}) collective-permute-start(bf16[32,64]{1,0:T(8,128)(2,1)S(1)} %collective-permute-done.1), channel_id=1, source_target_pairs={{0,1},{1,0},{2,3},{3,2},{4,5},{5,4},{6,7},{7,6},{8,9},{9,8},{10,11... | collective-permute-start | bytes 12296 | tf_op jit(solution)/shard_map/ppermute | solution.py:18
  30.1 9.5 %collective-permute-start.3 = (bf16[32,64]{1,0:T(8,128)(2,1)S(1)}, bf16[32,64]{1,0:T(8,128)(2,1)S(1)}, u32[]{:S(2)}, u32[]{:S(2)}) collective-permute-start(bf16[32,64]{1,0:T(8,128)(2,1)S(1)} %broadcast_select_fusion.5), channel_id=1, source_target_pairs={{0,64},{64,0},{16,80},{80,16},{32,96},{96,32},{48,112},{112,48},{1... | collective-permute-start | bytes 12296 | tf_op jit(solution)/shard_map/ppermute | solution.py:18
  41.3 3.7 %collective-permute-start.4 = (bf16[32,64]{1,0:T(8,128)(2,1)S(1)}, bf16[32,64]{1,0:T(8,128)(2,1)S(1)}, u32[]{:S(2)}, u32[]{:S(2)}) collective-permute-start(bf16[32,64]{1,0:T(8,128)(2,1)S(1)} %collective-permute-done.3), channel_id=1, source_target_pairs={{0,2},{2,0},{1,3},{3,1},{4,6},{6,4},{5,7},{7,5},{8,10},{10,8},{9,1... | collective-permute-start | bytes 12296 | tf_op jit(solution)/shard_map/ppermute | solution.py:18
  46.9 3.4 %collective-permute-start.5 = (bf16[32,64]{1,0:T(8,128)(2,1)S(1)}, bf16[32,64]{1,0:T(8,128)(2,1)S(1)}, u32[]{:S(2)}, u32[]{:S(2)}) collective-permute-start(bf16[32,64]{1,0:T(8,128)(2,1)S(1)} %broadcast_select_fusion.6), channel_id=1, source_target_pairs={{0,128},{128,0},{16,144},{144,16},{32,160},{160,32},{48,176},{176,... | collective-permute-start | bytes 12296 | tf_op jit(solution)/shard_map/ppermute | solution.py:18
  50.3 2.2 collective-permute-done.5
  52.4 4.3 %collective-permute-start.6 = (bf16[32,64]{1,0:T(8,128)(2,1)S(1)}, bf16[32,64]{1,0:T(8,128)(2,1)S(1)}, u32[]{:S(2)}, u32[]{:S(2)}) collective-permute-start(bf16[32,64]{1,0:T(8,128)(2,1)S(1)} %collective-permute-done.5), channel_id=1, source_target_pairs={{0,4},{4,0},{1,5},{5,1},{2,6},{6,2},{3,7},{7,3},{8,12},{12,8},{9,1... | collective-permute-start | bytes 12296 | tf_op jit(solution)/shard_map/ppermute | solution.py:18
  56.8 2.0 collective-permute-done.6
  58.9 4.9 %collective-permute-start.7 = (bf16[32,64]{1,0:T(8,128)(2,1)S(1)}, bf16[32,64]{1,0:T(8,128)(2,1)S(1)}, u32[]{:S(2)}, u32[]{:S(2)}) collective-permute-start(bf16[32,64]{1,0:T(8,128)(2,1)S(1)} %broadcast_select_fusion.7), channel_id=1, source_target_pairs={{0,256},{256,0},{16,272},{272,16},{32,288},{288,32},{48,304},{304,... | collective-permute-start | bytes 12296 | tf_op jit(solution)/shard_map/ppermute | solution.py:18
  63.7 2.2 collective-permute-done.7
  65.9 4.4 %collective-permute-start.8 = (bf16[32,64]{1,0:T(8,128)(2,1)S(1)}, bf16[32,64]{1,0:T(8,128)(2,1)S(1)}, u32[]{:S(2)}, u32[]{:S(2)}) collective-permute-start(bf16[32,64]{1,0:T(8,128)(2,1)S(1)} %collective-permute-done.7), channel_id=1, source_target_pairs={{0,8},{8,0},{1,9},{9,1},{2,10},{10,2},{3,11},{11,3},{4,12},{12,4},... | collective-permute-start | bytes 12296 | tf_op jit(solution)/shard_map/ppermute | solution.py:18
  71.9 3.5 %collective-permute-done.8 = bf16[32,64]{1,0:T(8,128)(2,1)S(1)} collective-permute-done((bf16[32,64]{1,0:T(8,128)(2,1)S(1)}, bf16[32,64]{1,0:T(8,128)(2,1)S(1)}, u32[]{:S(2)}, u32[]{:S(2)}) %collective-permute-start.8) | collective-permute-done | bytes 4128 | tf_op jit(solution)/shard_map/ppermute | solution.py:18
  75.4 48.4 %all-gather = bf16[32,64,32]{1,2,0:T(8,128)(2,1)S(1)} all-gather(bf16[1,64,32]{1,2,0:T(8,128)(2,1)S(1)} %select_bitcast_fusion.1), channel_id=1, replica_groups=mesh['row'=32,'col'=16] {'row'}, dimensions={0}, use_global_device_ids=true | all-gather | bytes 135168 | tf_op jit(solution)/shard_map/all_gather | solution.py:126
  124.8 19.2 %while.15 = (s32[]{:T(128)}, f32[16,4,32]{2,1,0:T(4,128)S(1)}, f32[16,4,32]{2,1,0:T(4,128)S(1)}, f32[16,4,32,32]{3,2,1,0:T(8,128)S(1)}, bf16[4,16,128,128]{3,2,0...) while((s32[]{:T(128)}, f32[16,4,32]{2,1,0:T(4,128)S(1)}, ...), condition=%wide.region_5.6_spmd.clone, body=%wide.region_2.5_spmd.clone.sunk | while | flops 170092544 | bytes 12550281 | solution.py:94
  146.1 2.2 collective-permute-start.9
  149.3 1.9 collective-permute-start.10
  151.2 9.4 %collective-permute-done.10 = bf16[32,2048]{1,0:T(8,128)(2,1)S(1)} collective-permute-done((bf16[32,2048]{1,0:T(8,128)(2,1)S(1)}, bf16[32,2048]{1,0:T(8,128)(2,1)S(1)}, u32[]{:S(2)}, u32[]{:S(2)}) %collective-permute-start.10) | collective-permute-done | bytes 131104 | tf_op jit(solution)/shard_map/ppermute | solution.py:18
  160.6 1.9 collective-permute-start.11
  162.5 5.2 %collective-permute-done.11 = bf16[32,2048]{1,0:T(8,128)(2,1)S(1)} collective-permute-done((bf16[32,2048]{1,0:T(8,128)(2,1)S(1)}, bf16[32,2048]{1,0:T(8,128)(2,1)S(1)}, u32[]{:S(2)}, u32[]{:S(2)}) %collective-permute-start.11) | collective-permute-done | bytes 131104 | tf_op jit(solution)/shard_map/ppermute | solution.py:18
  167.8 2.2 collective-permute-start.12
  170.0 8.6 %collective-permute-done.12 = bf16[32,2048]{1,0:T(8,128)(2,1)S(1)} collective-permute-done((bf16[32,2048]{1,0:T(8,128)(2,1)S(1)}, bf16[32,2048]{1,0:T(8,128)(2,1)S(1)}, u32[]{:S(2)}, u32[]{:S(2)}) %collective-permute-start.12) | collective-permute-done | bytes 131104 | tf_op jit(solution)/shard_map/ppermute | solution.py:18
  178.5 2.9 %collective-permute-start.13 = (bf16[32,2048]{1,0:T(8,128)(2,1)S(1)}, bf16[32,2048]{1,0:T(8,128)(2,1)S(1)}, u32[]{:S(2)}, u32[]{:S(2)}) collective-permute-start(bf16[32,2048]{1,0:T(8,128)(2,1)S(1)} %collective-permute-done.12), channel_id=1, source_target_pairs={{0,2},{2,0},{1,3},{3,1},{4,6},{6,4},{5,7},{7,5},{8,10},{10,8},{9,1... | collective-permute-start | bytes 393224 | tf_op jit(solution)/shard_map/ppermute | solution.py:18
  181.5 3.9 %collective-permute-done.13 = bf16[32,2048]{1,0:T(8,128)(2,1)S(1)} collective-permute-done((bf16[32,2048]{1,0:T(8,128)(2,1)S(1)}, bf16[32,2048]{1,0:T(8,128)(2,1)S(1)}, u32[]{:S(2)}, u32[]{:S(2)}) %collective-permute-start.13) | collective-permute-done | bytes 131104 | tf_op jit(solution)/shard_map/ppermute | solution.py:18
  185.4 1.9 collective-permute-start.14
  187.3 4.9 %collective-permute-done.14 = bf16[32,2048]{1,0:T(8,128)(2,1)S(1)} collective-permute-done((bf16[32,2048]{1,0:T(8,128)(2,1)S(1)}, bf16[32,2048]{1,0:T(8,128)(2,1)S(1)}, u32[]{:S(2)}, u32[]{:S(2)}) %collective-permute-start.14) | collective-permute-done | bytes 131104 | tf_op jit(solution)/shard_map/ppermute | solution.py:18
  192.3 4.2 %collective-permute-start.15 = (bf16[32,2048]{1,0:T(8,128)(2,1)S(1)}, bf16[32,2048]{1,0:T(8,128)(2,1)S(1)}, u32[]{:S(2)}, u32[]{:S(2)}) collective-permute-start(bf16[32,2048]{1,0:T(8,128)(2,1)S(1)} %collective-permute-done.14), channel_id=1, source_target_pairs={{0,4},{4,0},{1,5},{5,1},{2,6},{6,2},{3,7},{7,3},{8,12},{12,8},{9,1... | collective-permute-start | bytes 393224 | tf_op jit(solution)/shard_map/ppermute | solution.py:18
  196.5 4.9 %collective-permute-done.15 = bf16[32,2048]{1,0:T(8,128)(2,1)S(1)} collective-permute-done((bf16[32,2048]{1,0:T(8,128)(2,1)S(1)}, bf16[32,2048]{1,0:T(8,128)(2,1)S(1)}, u32[]{:S(2)}, u32[]{:S(2)}) %collective-permute-start.15) | collective-permute-done | bytes 131104 | tf_op jit(solution)/shard_map/ppermute | solution.py:18
  201.4 1.9 collective-permute-start.16
  203.4 6.4 %collective-permute-done.16 = bf16[32,2048]{1,0:T(8,128)(2,1)S(1)} collective-permute-done((bf16[32,2048]{1,0:T(8,128)(2,1)S(1)}, bf16[32,2048]{1,0:T(8,128)(2,1)S(1)}, u32[]{:S(2)}, u32[]{:S(2)}) %collective-permute-start.16) | collective-permute-done | bytes 131104 | tf_op jit(solution)/shard_map/ppermute | solution.py:18
  209.8 3.6 %collective-permute-start.17 = (bf16[32,2048]{1,0:T(8,128)(2,1)S(1)}, bf16[32,2048]{1,0:T(8,128)(2,1)S(1)}, u32[]{:S(2)}, u32[]{:S(2)}) collective-permute-start(bf16[32,2048]{1,0:T(8,128)(2,1)S(1)} %collective-permute-done.16), channel_id=1, source_target_pairs={{0,8},{8,0},{1,9},{9,1},{2,10},{10,2},{3,11},{11,3},{4,12},{12,4},... | collective-permute-start | bytes 393224 | tf_op jit(solution)/shard_map/ppermute | solution.py:18
  213.4 8.1 %collective-permute-done.17 = bf16[32,2048]{1,0:T(8,128)(2,1)S(1)} collective-permute-done((bf16[32,2048]{1,0:T(8,128)(2,1)S(1)}, bf16[32,2048]{1,0:T(8,128)(2,1)S(1)}, u32[]{:S(2)}, u32[]{:S(2)}) %collective-permute-start.17) | collective-permute-done | bytes 131104 | tf_op jit(solution)/shard_map/ppermute | solution.py:18
  (117 shorter events, 38.9 us)
Async XLA Ops:
  7.2 63.2 %copy-start = (bf16[128,128]{1,0:T(8,128)(2,1)S(1)}, bf16[128,128]{1,0:T(8,128)(2,1)}, u32[]{:S(2)}) copy-start(bf16[128,128]{1,0:T(8,128)(2,1)} %param.12) | copy-start | bytes 98308
  7.2 117.6 %all-gather.3.cloned.1.call-start = ((), (), s32[]{:S(2)}) async-start(), calls=%async_computation | async-start | bytes 2228224 | tf_op jit(solution)/shard_map/all_gather | solution.py:145
  13.4 3.1 %collective-permute-start = (bf16[16,64]{1,0:T(8,128)(2,1)S(1)}, bf16[16,64]{1,0:T(8,128)(2,1)S(1)}, u32[]{:S(2)}, u32[]{:S(2)}) collective-permute-start(bf16[16,64]{1,0:T(8,128)(2,1)S(1)} %get-tuple-element.149), channel_id=1, source_target_pairs={{0,16},{16,0},{32,48},{48,32},{64,80},{80,64},{96,112},{112,96},{1... | collective-permute-start | bytes 6152 | tf_op jit(solution)/shard_map/ppermute | solution.py:18
  16.5 7.7 %collective-permute-start.1 = (bf16[32,64]{1,0:T(8,128)(2,1)S(1)}, bf16[32,64]{1,0:T(8,128)(2,1)S(1)}, u32[]{:S(2)}, u32[]{:S(2)}) collective-permute-start(bf16[32,64]{1,0:T(8,128)(2,1)S(1)} %maximum_select_fusion.1), channel_id=1, source_target_pairs={{0,32},{32,0},{16,48},{48,16},{64,96},{96,64},{80,112},{112,80},{1... | collective-permute-start | bytes 12296 | tf_op jit(solution)/shard_map/ppermute | solution.py:18
  24.2 5.9 %collective-permute-start.2 = (bf16[32,64]{1,0:T(8,128)(2,1)S(1)}, bf16[32,64]{1,0:T(8,128)(2,1)S(1)}, u32[]{:S(2)}, u32[]{:S(2)}) collective-permute-start(bf16[32,64]{1,0:T(8,128)(2,1)S(1)} %collective-permute-done.1), channel_id=1, source_target_pairs={{0,1},{1,0},{2,3},{3,2},{4,5},{5,4},{6,7},{7,6},{8,9},{9,8},{10,11... | collective-permute-start | bytes 12296 | tf_op jit(solution)/shard_map/ppermute | solution.py:18
  30.1 11.2 %collective-permute-start.3 = (bf16[32,64]{1,0:T(8,128)(2,1)S(1)}, bf16[32,64]{1,0:T(8,128)(2,1)S(1)}, u32[]{:S(2)}, u32[]{:S(2)}) collective-permute-start(bf16[32,64]{1,0:T(8,128)(2,1)S(1)} %broadcast_select_fusion.5), channel_id=1, source_target_pairs={{0,64},{64,0},{16,80},{80,16},{32,96},{96,32},{48,112},{112,48},{1... | collective-permute-start | bytes 12296 | tf_op jit(solution)/shard_map/ppermute | solution.py:18
  41.3 5.5 %collective-permute-start.4 = (bf16[32,64]{1,0:T(8,128)(2,1)S(1)}, bf16[32,64]{1,0:T(8,128)(2,1)S(1)}, u32[]{:S(2)}, u32[]{:S(2)}) collective-permute-start(bf16[32,64]{1,0:T(8,128)(2,1)S(1)} %collective-permute-done.3), channel_id=1, source_target_pairs={{0,2},{2,0},{1,3},{3,1},{4,6},{6,4},{5,7},{7,5},{8,10},{10,8},{9,1... | collective-permute-start | bytes 12296 | tf_op jit(solution)/shard_map/ppermute | solution.py:18
  46.9 5.5 %collective-permute-start.5 = (bf16[32,64]{1,0:T(8,128)(2,1)S(1)}, bf16[32,64]{1,0:T(8,128)(2,1)S(1)}, u32[]{:S(2)}, u32[]{:S(2)}) collective-permute-start(bf16[32,64]{1,0:T(8,128)(2,1)S(1)} %broadcast_select_fusion.6), channel_id=1, source_target_pairs={{0,128},{128,0},{16,144},{144,16},{32,160},{160,32},{48,176},{176,... | collective-permute-start | bytes 12296 | tf_op jit(solution)/shard_map/ppermute | solution.py:18
  52.4 6.4 %collective-permute-start.6 = (bf16[32,64]{1,0:T(8,128)(2,1)S(1)}, bf16[32,64]{1,0:T(8,128)(2,1)S(1)}, u32[]{:S(2)}, u32[]{:S(2)}) collective-permute-start(bf16[32,64]{1,0:T(8,128)(2,1)S(1)} %collective-permute-done.5), channel_id=1, source_target_pairs={{0,4},{4,0},{1,5},{5,1},{2,6},{6,2},{3,7},{7,3},{8,12},{12,8},{9,1... | collective-permute-start | bytes 12296 | tf_op jit(solution)/shard_map/ppermute | solution.py:18
  58.9 7.0 %collective-permute-start.7 = (bf16[32,64]{1,0:T(8,128)(2,1)S(1)}, bf16[32,64]{1,0:T(8,128)(2,1)S(1)}, u32[]{:S(2)}, u32[]{:S(2)}) collective-permute-start(bf16[32,64]{1,0:T(8,128)(2,1)S(1)} %broadcast_select_fusion.7), channel_id=1, source_target_pairs={{0,256},{256,0},{16,272},{272,16},{32,288},{288,32},{48,304},{304,... | collective-permute-start | bytes 12296 | tf_op jit(solution)/shard_map/ppermute | solution.py:18
  65.9 9.5 %collective-permute-start.8 = (bf16[32,64]{1,0:T(8,128)(2,1)S(1)}, bf16[32,64]{1,0:T(8,128)(2,1)S(1)}, u32[]{:S(2)}, u32[]{:S(2)}) collective-permute-start(bf16[32,64]{1,0:T(8,128)(2,1)S(1)} %collective-permute-done.7), channel_id=1, source_target_pairs={{0,8},{8,0},{1,9},{9,1},{2,10},{10,2},{3,11},{11,3},{4,12},{12,4},... | collective-permute-start | bytes 12296 | tf_op jit(solution)/shard_map/ppermute | solution.py:18
  71.5 53.3 %copy-start.2 = (bf16[128,128]{1,0:T(8,128)(2,1)S(1)}, bf16[128,128]{1,0:T(8,128)(2,1)}, u32[]{:S(2)}) copy-start(bf16[128,128]{1,0:T(8,128)(2,1)} %param.13) | copy-start | bytes 98308
  71.5 53.3 %copy-start.3 = (bf16[128,128]{1,0:T(8,128)(2,1)S(1)}, bf16[128,128]{1,0:T(8,128)(2,1)}, u32[]{:S(2)}) copy-start(bf16[128,128]{1,0:T(8,128)(2,1)} %param.14) | copy-start | bytes 98308
  144.4 1.2 copy-start.1
  144.4 1.2 copy-start.5
  144.4 1.2 copy-start.6
  146.0 76.3 %copy-start.4 = (bf16[512,128]{1,0:T(8,128)(2,1)}, bf16[512,128]{1,0:T(8,128)(2,1)S(1)}, u32[]{:S(2)}) copy-start(bf16[512,128]{1,0:T(8,128)(2,1)S(1)} %convolution_convert_fusion.2) | copy-start | bytes 393220
  146.1 3.1 %collective-permute-start.9 = (bf16[16,2048]{1,0:T(8,128)(2,1)S(1)}, bf16[16,2048]{1,0:T(8,128)(2,1)S(1)}, u32[]{:S(2)}, u32[]{:S(2)}) collective-permute-start(bf16[16,2048]{1,0:T(8,128)(2,1)S(1)} %get-tuple-element.147), channel_id=1, source_target_pairs={{0,16},{16,0},{32,48},{48,32},{64,80},{80,64},{96,112},{112,96},{1... | collective-permute-start | bytes 196616 | tf_op jit(solution)/shard_map/ppermute | solution.py:18
  149.3 11.3 %collective-permute-start.10 = (bf16[32,2048]{1,0:T(8,128)(2,1)S(1)}, bf16[32,2048]{1,0:T(8,128)(2,1)S(1)}, u32[]{:S(2)}, u32[]{:S(2)}) collective-permute-start(bf16[32,2048]{1,0:T(8,128)(2,1)S(1)} %maximum_select_fusion), channel_id=1, source_target_pairs={{0,32},{32,0},{16,48},{48,16},{64,96},{96,64},{80,112},{112,80},{1... | collective-permute-start | bytes 393224 | tf_op jit(solution)/shard_map/ppermute | solution.py:18
  160.6 7.1 %collective-permute-start.11 = (bf16[32,2048]{1,0:T(8,128)(2,1)S(1)}, bf16[32,2048]{1,0:T(8,128)(2,1)S(1)}, u32[]{:S(2)}, u32[]{:S(2)}) collective-permute-start(bf16[32,2048]{1,0:T(8,128)(2,1)S(1)} %collective-permute-done.10), channel_id=1, source_target_pairs={{0,1},{1,0},{2,3},{3,2},{4,5},{5,4},{6,7},{7,6},{8,9},{9,8},{10,11... | collective-permute-start | bytes 393224 | tf_op jit(solution)/shard_map/ppermute | solution.py:18
  167.8 10.8 %collective-permute-start.12 = (bf16[32,2048]{1,0:T(8,128)(2,1)S(1)}, bf16[32,2048]{1,0:T(8,128)(2,1)S(1)}, u32[]{:S(2)}, u32[]{:S(2)}) collective-permute-start(bf16[32,2048]{1,0:T(8,128)(2,1)S(1)} %broadcast_select_fusion), channel_id=1, source_target_pairs={{0,64},{64,0},{16,80},{80,16},{32,96},{96,32},{48,112},{112,48},{1... | collective-permute-start | bytes 393224 | tf_op jit(solution)/shard_map/ppermute | solution.py:18
  178.5 6.8 %collective-permute-start.13 = (bf16[32,2048]{1,0:T(8,128)(2,1)S(1)}, bf16[32,2048]{1,0:T(8,128)(2,1)S(1)}, u32[]{:S(2)}, u32[]{:S(2)}) collective-permute-start(bf16[32,2048]{1,0:T(8,128)(2,1)S(1)} %collective-permute-done.12), channel_id=1, source_target_pairs={{0,2},{2,0},{1,3},{3,1},{4,6},{6,4},{5,7},{7,5},{8,10},{10,8},{9,1... | collective-permute-start | bytes 393224 | tf_op jit(solution)/shard_map/ppermute | solution.py:18
  185.4 6.9 %collective-permute-start.14 = (bf16[32,2048]{1,0:T(8,128)(2,1)S(1)}, bf16[32,2048]{1,0:T(8,128)(2,1)S(1)}, u32[]{:S(2)}, u32[]{:S(2)}) collective-permute-start(bf16[32,2048]{1,0:T(8,128)(2,1)S(1)} %broadcast_select_fusion.1), channel_id=1, source_target_pairs={{0,128},{128,0},{16,144},{144,16},{32,160},{160,32},{48,176},{176,... | collective-permute-start | bytes 393224 | tf_op jit(solution)/shard_map/ppermute | solution.py:18
  192.3 9.2 %collective-permute-start.15 = (bf16[32,2048]{1,0:T(8,128)(2,1)S(1)}, bf16[32,2048]{1,0:T(8,128)(2,1)S(1)}, u32[]{:S(2)}, u32[]{:S(2)}) collective-permute-start(bf16[32,2048]{1,0:T(8,128)(2,1)S(1)} %collective-permute-done.14), channel_id=1, source_target_pairs={{0,4},{4,0},{1,5},{5,1},{2,6},{6,2},{3,7},{7,3},{8,12},{12,8},{9,1... | collective-permute-start | bytes 393224 | tf_op jit(solution)/shard_map/ppermute | solution.py:18
  201.4 8.4 %collective-permute-start.16 = (bf16[32,2048]{1,0:T(8,128)(2,1)S(1)}, bf16[32,2048]{1,0:T(8,128)(2,1)S(1)}, u32[]{:S(2)}, u32[]{:S(2)}) collective-permute-start(bf16[32,2048]{1,0:T(8,128)(2,1)S(1)} %broadcast_select_fusion.2), channel_id=1, source_target_pairs={{0,256},{256,0},{16,272},{272,16},{32,288},{288,32},{48,304},{304,... | collective-permute-start | bytes 393224 | tf_op jit(solution)/shard_map/ppermute | solution.py:18
  209.8 11.8 %collective-permute-start.17 = (bf16[32,2048]{1,0:T(8,128)(2,1)S(1)}, bf16[32,2048]{1,0:T(8,128)(2,1)S(1)}, u32[]{:S(2)}, u32[]{:S(2)}) collective-permute-start(bf16[32,2048]{1,0:T(8,128)(2,1)S(1)} %collective-permute-done.16), channel_id=1, source_target_pairs={{0,8},{8,0},{1,9},{9,1},{2,10},{10,2},{3,11},{11,3},{4,12},{12,4},... | collective-permute-start | bytes 393224 | tf_op jit(solution)/shard_map/ppermute | solution.py:18
Sparse Core Ops, SparseCore 0:
  12.0 78.6 all-gather.2
where the time goes:
time: 230 us; the launch traced here: 229 us
  waiting for transfers between devices  70.2 us (31%)
  starting transfers between devices  65.3 us (28%)
  blocking collectives  48.4 us (21%)
  between operations  14.8 us (6%)
  matrix products  11.2 us (5%)
  local copies, waits for them, and re-layouts  10.6 us (5%)
  other arithmetic  8.28 us (4%)
    ppermute x18, waiting for transfers between devices, partner(): return lax.ppermute(block, axis, route)  70.2 us
    ppermute x18, starting transfers between devices, partner(): return lax.ppermute(block, axis, route)  65.3 us
    all_gather x1, blocking collectives, per_device(): bias_rows = lax.all_gather(mirrored, 'row', axis=1, tiled=True)  48.4 us
    dot_general x11, matrix products, project(): return jnp.dot(flat_rows, weight, preferred_element_type=jnp.float32)  4.67 us
  transfers between devices with their start and end apart: 19, of which 18 were waited for; matrix products, arithmetic and copies ran while one was open for 2% of the time, Pallas kernels for 0%

commit v1 on v0

v1 whole, which is shorter than its diff:
```python
import jax
import jax.numpy as jnp
from jax import lax
from jax.experimental import pallas as pl
from jax.experimental.pallas import tpu as pltpu
from jax.sharding import PartitionSpec as P

EPSILON = 1e-05
MESH = pl.DeviceIdType.MESH
NT = (((1,), (1,)), ((), ()))


def dot(a, b):
    return jnp.dot(a, b, preferred_element_type=jnp.float32)


def dot_nt(a, b):
    return lax.dot_general(a, b, NT, preferred_element_type=jnp.float32)


def kernel(
    pair_ref,
    gain_ref,
    wq_ref,
    wk_ref,
    wv_ref,
    wg_ref,
    bw_ref,
    wo_ref,
    upd_ref,
    mir_ref,
    nrm,
    xcat,
    wbd,
    b1buf,
    bbuf,
    biasf,
    xall,
    kbuf,
    vbuf,
    qbuf,
    gbuf,
    xq,
    ustage,
    ufull,
    mstage,
    mflat,
    s1_s,
    s1_r,
    s2_s,
    s2_r,
    b1_s,
    b1_r,
    b2_s,
    b2_r,
    b3_s,
    b3_r,
    o1_s,
    o1_r,
    o2_s,
    o2_r,
    m_s,
    m_r,
):
    r = lax.axis_index("row")
    c = lax.axis_index("col")
    x = r // 8
    zh = (r // 2) % 4
    core = r % 2
    y = c // 2
    zl = c % 2
    z = zh * 2 + zl
    sibling = (r + 1 - 2 * core, c)

    def col_peer(k):
        return (r, (c + k) % 16)

    def x_row(xx):
        return xx * 8 + zh * 2 + core

    def y_peer(k):
        return (r, ((y + k) % 8) * 2 + zl)

    def z_peer(k):
        zz = (z + k) % 8
        return (x * 8 + (zz // 2) * 2 + core, y * 2 + zz % 2)

    def send(src, dst, s_sem, r_sem, dev):
        pltpu.make_async_remote_copy(
            src_ref=src,
            dst_ref=dst,
            send_sem=s_sem,
            recv_sem=r_sem,
            device_id=dev,
            device_id_type=MESH,
        ).start()

    def arrived(ref, sem):
        pltpu.make_async_copy(ref, ref, sem).wait()

    def loop(low, high, body):
        def step(k, carry):
            body(k)
            return carry

        lax.fori_loop(low, high, step, 0)

    barrier = pltpu.get_barrier_semaphore()

    def greet(dev):
        pl.semaphore_signal(barrier, inc=1, device_id=dev, device_id_type=MESH)

    loop(1, 16, lambda k: greet(col_peer(k)))
    loop(1, 8, lambda k: greet(z_peer(k)))
    loop(1, 4, lambda k: greet((x_row((x + k) % 4), c)))
    greet(sibling)

    entries = pair_ref[...].reshape(512, 128).astype(jnp.float32)
    center = jnp.mean(entries, axis=-1, keepdims=True)
    shifted = entries - center
    spread = jnp.mean(shifted * shifted, axis=-1, keepdims=True)
    gain = gain_ref[...].astype(jnp.float32)
    normed = (shifted * lax.rsqrt(spread + EPSILON) * gain).astype(jnp.bfloat16)
    nrm[...] = normed.reshape(16, 32, 128)

    xcat[...] = jnp.zeros_like(xcat)
    place = pl.multiple_of((y % 4) * 32, 32)
    for j in range(16):
        xcat[pl.ds(place, 32), j * 128 : (j + 1) * 128] = nrm[j]
    heads = lax.broadcasted_iota(jnp.int32, (64, 4), 0) // 16
    pick = heads == lax.broadcasted_iota(jnp.int32, (64, 4), 1)
    spread_w = dot_nt(pick.astype(jnp.float32).astype(jnp.bfloat16), bw_ref[...])
    row_j = lax.broadcasted_iota(jnp.int32, (64, 128), 0) % 16
    for j in range(16):
        wbd[:, j * 128 : (j + 1) * 128] = jnp.where(row_j == j, spread_w, 0.0).astype(
            jnp.bfloat16
        )
    b1buf[y] = dot_nt(wbd[...], xcat[...]).astype(jnp.bfloat16)

    pl.semaphore_wait(barrier, 26)

    loop(
        1,
        8,
        lambda k: send(b1buf.at[y], b1buf.at[y], b1_s.at[k], b1_r.at[k], y_peer(k)),
    )
    own_slot = pl.multiple_of((zl * 8 + y) * 32, 32)
    loop(
        1,
        16,
        lambda k: send(
            nrm.at[(c + k) % 16],
            xall.at[0, pl.ds(own_slot, 32)],
            s1_s.at[k],
            s1_r.at[k],
            col_peer(k),
        ),
    )
    xall[0, pl.ds(own_slot, 32)] = nrm[c]

    loop(1, 8, lambda k: arrived(b1buf.at[0], b1_r.at[k]))
    for g in range(2):
        merged = b1buf[4 * g].astype(jnp.float32)
        for i in range(1, 4):
            merged = merged + b1buf[4 * g + i].astype(jnp.float32)
        bbuf[core, z, :, g * 128 : (g + 1) * 128] = merged.astype(jnp.bfloat16)
    own_bias = bbuf.at[core, z]
    loop(1, 8, lambda k: send(own_bias, own_bias, b2_s.at[k], b2_r.at[k], z_peer(k)))
    send(own_bias, own_bias, b3_s.at[0], b3_r.at[0], sibling)

    loop(1, 16, lambda k: arrived(xall.at[0, pl.ds(0, 32)], s1_r.at[k]))
    loop(
        1,
        4,
        lambda d: send(
            xall.at[0], xall.at[d], s2_s.at[d], s2_r.at[d], (x_row((x + d) % 4), c)
        ),
    )

    def project(d):
        keys = xall[d]
        kbuf[d] = dot(keys, wk_ref[...]).astype(jnp.bfloat16)
        vbuf[d] = dot(keys, wv_ref[...]).astype(jnp.bfloat16)
        for q in range(4):
            slot = pl.multiple_of(((q % 2) * 8 + 2 * x + q // 2) * 32, 32)
            xq[q * 32 : (q + 1) * 32] = xall[d, pl.ds(slot, 32)]
        own = xq[...]
        qbuf[d] = (dot(own, wq_ref[...]) * 32**-0.5).astype(jnp.bfloat16)
        gbuf[d] = jax.nn.sigmoid(dot(own, wg_ref[...]))

    project(0)

    def forward(k):
        zz = (z - k + 8) % 8
        block = bbuf.at[core, zz]
        arrived(block, b2_r.at[k])
        send(block, block, b3_s.at[k], b3_r.at[k], sibling)

    loop(1, 8, forward)

    def next_row(d):
        arrived(xall.at[d], s2_r.at[d])
        project(d)

    loop(1, 4, next_row)

    loop(0, 8, lambda k: arrived(bbuf.at[0, 0], b3_r.at[k]))
    for half in range(2):
        for zz in range(8):
            j0 = ((zz // 2) * 2 + half) * 16
            k0 = (zz % 2) * 256
            block = bbuf[half, zz].astype(jnp.float32)
            for h in range(4):
                biasf[h, j0 : j0 + 16, k0 : k0 + 256] = block[h * 16 : (h + 1) * 16]

    head_of_lane = lax.broadcasted_iota(jnp.int32, (128, 128), 1) // 32

    def attend(d):
        queries = qbuf[d].astype(jnp.float32)
        attended = jnp.zeros((128, 128), jnp.float32)
        for h in range(4):
            mine = jnp.where(head_of_lane == h, queries, 0.0).astype(jnp.bfloat16)
            scores = dot_nt(mine, kbuf[d]) + biasf[h]
            exponent = jnp.exp(scores - jnp.max(scores, axis=-1, keepdims=True))
            denominator = jnp.sum(exponent, axis=-1, keepdims=True)
            mixed = dot(exponent.astype(jnp.bfloat16), vbuf[d])
            attended = jnp.where(head_of_lane == h, mixed / denominator, attended)
        gated = (gbuf[d] * attended).astype(jnp.bfloat16)
        ustage[d] = dot(gated, wo_ref[...]).astype(jnp.bfloat16)

    def mirror_copy(d, t):
        x_i = (x - d + 4) % 4
        to_row = x * 8 + t
        to_col = x_i * 4 + zh
        src = ustage.at[d, pl.ds(pl.multiple_of(t * 16, 16), 16)]
        dst = mstage.at[core * 16 + c]
        r_sem = m_r.at[core * 16 + c]
        here = jnp.logical_and(to_row == r, to_col == c)
        s_sem = m_s.at[d * 8 + t]
        return src, dst, s_sem, r_sem, (to_row, to_col), here

    def emit(d):
        attend(d)
        x_i = (x - d + 4) % 4

        @pl.when(d > 0)
        def _():
            send(ustage.at[d], ufull.at[x], o1_s.at[d], o1_r.at[d], (x_row(x_i), c))

        def one(t):
            src, dst, s_sem, r_sem, dev, here = mirror_copy(d, t)

            @pl.when(here)
            def _():
                pltpu.make_async_copy(src, dst, r_sem).start()

            @pl.when(jnp.logical_not(here))
            def _():
                send(src, dst, s_sem, r_sem, dev)

        loop(0, 8, one)

    loop(0, 4, emit)
    ufull[x] = ustage[0]

    loop(1, 4, lambda d: arrived(ufull.at[0], o1_r.at[d]))

    def give(k):
        cc = (c + k) % 16
        rows = pl.ds(pl.multiple_of((cc % 4) * 32, 32), 32)
        send(
            ufull.at[cc // 4, rows], upd_ref.at[c], o2_s.at[k], o2_r.at[k], col_peer(k)
        )

    loop(1, 16, give)
    upd_ref[c] = ufull[c // 4, pl.ds(pl.multiple_of((c % 4) * 32, 32), 32)]

    loop(1, 8, lambda k: arrived(b1buf.at[0], b1_s.at[k]))
    loop(1, 16, lambda k: arrived(nrm.at[0], s1_s.at[k]))
    loop(1, 8, lambda k: arrived(bbuf.at[0, 0], b2_s.at[k]))
    loop(0, 8, lambda k: arrived(bbuf.at[0, 0], b3_s.at[k]))
    loop(1, 4, lambda d: arrived(xall.at[0], s2_s.at[d]))
    loop(1, 4, lambda d: arrived(ustage.at[0], o1_s.at[d]))

    loop(0, 32, lambda k: arrived(mstage.at[0], m_r.at[k]))
    mflat[...] = mstage[...].astype(jnp.float32).reshape(512, 128)
    for j in range(16):
        mir_ref[j] = mflat[pl.ds(j, 32, stride=16), :].astype(jnp.bfloat16)

    def mirror_left(d):
        def one(t):
            src, dst, s_sem, r_sem, dev, here = mirror_copy(d, t)

            @pl.when(jnp.logical_not(here))
            def _():
                arrived(src, s_sem)

        loop(0, 8, one)

    loop(0, 4, mirror_left)
    loop(1, 16, lambda k: arrived(upd_ref.at[0], o2_r.at[k]))
    loop(1, 16, lambda k: arrived(upd_ref.at[0], o2_s.at[k]))


def per_device(pair, gain, wq, wk, wv, wg, bw, wo):
    bf16, f32 = jnp.bfloat16, jnp.float32
    vmem = pl.BlockSpec(memory_space=pltpu.VMEM)
    dma = pltpu.SemaphoreType.DMA
    tile = jax.ShapeDtypeStruct(pair.shape, bf16)
    return pl.pallas_call(
        kernel,
        out_shape=(tile, tile),
        in_specs=[vmem] * 8,
        out_specs=(vmem, vmem),
        scratch_shapes=[
            pltpu.VMEM((16, 32, 128), bf16),
            pltpu.VMEM((128, 2048), bf16),
            pltpu.VMEM((64, 2048), bf16),
            pltpu.VMEM((8, 64, 128), bf16),
            pltpu.VMEM((2, 8, 64, 256), bf16),
            pltpu.VMEM((4, 128, 512), f32),
            pltpu.VMEM((4, 512, 128), bf16),
            pltpu.VMEM((4, 512, 128), bf16),
            pltpu.VMEM((4, 512, 128), bf16),
            pltpu.VMEM((4, 128, 128), bf16),
            pltpu.VMEM((4, 128, 128), f32),
            pltpu.VMEM((128, 128), bf16),
            pltpu.VMEM((4, 128, 128), bf16),
            pltpu.VMEM((4, 128, 128), bf16),
            pltpu.VMEM((32, 16, 128), bf16),
            pltpu.VMEM((512, 128), f32),
            dma((16,)),
            dma((16,)),
            dma((4,)),
            dma((4,)),
            dma((8,)),
            dma((8,)),
            dma((8,)),
            dma((8,)),
            dma((8,)),
            dma((8,)),
            dma((4,)),
            dma((4,)),
            dma((16,)),
            dma((16,)),
            dma((32,)),
            dma((32,)),
        ],
        compiler_params=pltpu.CompilerParams(
            collective_id=0, has_side_effects=True, vmem_limit_bytes=48 * 2**20
        ),
        cost_estimate=pl.CostEstimate(
            flops=1_000_000_000, bytes_accessed=1_000_000, transcendentals=1_100_000
        ),
    )(pair, gain.reshape(1, 128), wq, wk, wv, wg, bw, wo)


def solution(mesh):
    placed = (P("row", "col", None), P(), P(), P(), P(), P(), P(), P())
    return jax.shard_map(
        per_device,
        mesh=mesh,
        in_specs=placed,
        out_specs=(P("row", "col", None), P("row", "col", None)),
        check_vma=False,
    )
```

time: 230 us -> 56.3 us (0.24)
  the two profiles are of different devices: /device:TPU:56 before, /device:TPU:1 now
where the time goes in v1:
time: 56.3 us; the launch traced here: 55.8 us
  Pallas kernels  48.6 us (86%)
  local copies, waits for them, and re-layouts  6.57 us (12%)
  between operations  0.66 us (1%)
    pallas_call x1, Pallas kernels, per_device(): pl.pallas_call(kernel, out_shape=(tile, tile), in_specs=[vmem] * 8, out_s...  48.6 us
    unnamed x19, local copies, waits for them, and re-layouts  6.57 us

profile of v1, /device:TPU:1, one launch (start us, length us, event | category | flops | bytes accessed | tf_op | source)
XLA Modules:
  0.0 55.8 jit_solution(15286870125059681301)
XLA Ops:
  0.6 0.0 copy-start.7
  0.6 0.0 copy-start.1
  0.7 0.7 %copy-done.7 = bf16[128,4]{0,1:T(4,128)(2,1)S(1)} copy-done((bf16[128,4]{0,1:T(4,128)(2,1)S(1)}, bf16[128,4]{0,1:T(4,128)(2,1)}, u32[]{:S(2)}) %copy-start.7) | copy-done | bytes 1048
  1.3 0.0 copy-start.6
  1.3 0.1 copy.10.bw_ref
  1.4 0.0 copy-done.1
  1.5 0.5 copy-done.6
  2.0 0.0 copy-start
  2.0 0.9 %copy-done = bf16[16,32,128]{2,1,0:T(8,128)(2,1)S(1)} copy-done((bf16[16,32,128]{2,1,0:T(8,128)(2,1)S(1)}, bf16[16,32,128]{2,1,0:T(8,128)(2,1)}, u32[]{:S(2)}) %copy-start) | copy-done | bytes 131096
  2.9 0.0 copy-start.2
  2.9 0.8 %copy-done.2 = bf16[128,128]{1,0:T(8,128)(2,1)S(1)} copy-done((bf16[128,128]{1,0:T(8,128)(2,1)S(1)}, bf16[128,128]{1,0:T(8,128)(2,1)}, u32[]{:S(2)}) %copy-start.2) | copy-done | bytes 32792
  3.6 0.0 copy-start.3
  3.6 0.8 %copy-done.3 = bf16[128,128]{1,0:T(8,128)(2,1)S(1)} copy-done((bf16[128,128]{1,0:T(8,128)(2,1)S(1)}, bf16[128,128]{1,0:T(8,128)(2,1)}, u32[]{:S(2)}) %copy-start.3) | copy-done | bytes 32792
  4.4 0.0 copy-start.4
  4.4 0.8 %copy-done.4 = bf16[128,128]{1,0:T(8,128)(2,1)S(1)} copy-done((bf16[128,128]{1,0:T(8,128)(2,1)S(1)}, bf16[128,128]{1,0:T(8,128)(2,1)}, u32[]{:S(2)}) %copy-start.4) | copy-done | bytes 32792
  5.2 0.0 copy-start.5
  5.2 0.8 %copy-done.5 = bf16[128,128]{1,0:T(8,128)(2,1)S(1)} copy-done((bf16[128,128]{1,0:T(8,128)(2,1)S(1)}, bf16[128,128]{1,0:T(8,128)(2,1)}, u32[]{:S(2)}) %copy-start.5) | copy-done | bytes 32792
  5.9 48.6 %shard_map.95 = (bf16[16,32,128]{2,1,0:T(8,128)(2,1)S(1)}, bf16[16,32,128]{2,1,0:T(8,128)(2,1)S(1)}) custom-call(bf16[16,32,128]{2,1,0:T(8,128)(2,1)S(1)} %copy-done, bf16[1,128]{1,0:T(2,128)(2,1)S(1)} %bitcast.1, bf16[128,128]{1,0:T(8,128)(2,1)S(1)} %copy-done.1, bf16[128,128]{1,0:T(8,128)(2,1)S(1)} %copy-done.2, bf16[128,128]{1,0:T(8,128)(2,1)S(1)} %copy-done.3, ...), custom_call_target="tpu_custom_call" | custom-call | flops 1000000000 | bytes 1000000 | tf_op jit(solution)/shard_map/pallas_call | solution.py:310
  54.5 0.7 %copy.13 = bf16[16,32,128]{2,1,0:T(8,128)(2,1)} copy(bf16[16,32,128]{2,1,0:T(8,128)(2,1)S(1)} %get-tuple-element.4) | data formatting | bytes 262144
  55.2 0.7 %copy.14 = bf16[16,32,128]{2,1,0:T(8,128)(2,1)} copy(bf16[16,32,128]{2,1,0:T(8,128)(2,1)S(1)} %get-tuple-element.5) | data formatting | bytes 262144
Async XLA Ops:
  0.6 0.7 %copy-start.7 = (bf16[128,4]{0,1:T(4,128)(2,1)S(1)}, bf16[128,4]{0,1:T(4,128)(2,1)}, u32[]{:S(2)}) copy-start(bf16[128,4]{0,1:T(4,128)(2,1)} %param.14) | copy-start | bytes 3076
  0.6 0.8 %copy-start.1 = (bf16[128,128]{1,0:T(8,128)(2,1)S(1)}, bf16[128,128]{1,0:T(8,128)(2,1)}, u32[]{:S(2)}) copy-start(bf16[128,128]{1,0:T(8,128)(2,1)} %wq_ref.1) | copy-start | bytes 98308
  1.3 0.7 %copy-start.6 = (bf16[128]{0:T(256)(128)(2,1)S(1)}, bf16[128]{0:T(256)(128)(2,1)}, u32[]{:S(2)}) copy-start(bf16[128]{0:T(256)(128)(2,1)} %param.9) | copy-start | bytes 772
  2.0 0.9 %copy-start = (bf16[16,32,128]{2,1,0:T(8,128)(2,1)S(1)}, bf16[16,32,128]{2,1,0:T(8,128)(2,1)}, u32[]{:S(2)}) copy-start(bf16[16,32,128]{2,1,0:T(8,128)(2,1)} %pair_ref.1) | copy-start | bytes 393220
  2.9 0.8 %copy-start.2 = (bf16[128,128]{1,0:T(8,128)(2,1)S(1)}, bf16[128,128]{1,0:T(8,128)(2,1)}, u32[]{:S(2)}) copy-start(bf16[128,128]{1,0:T(8,128)(2,1)} %wk_ref.1) | copy-start | bytes 98308
  3.6 0.8 %copy-start.3 = (bf16[128,128]{1,0:T(8,128)(2,1)S(1)}, bf16[128,128]{1,0:T(8,128)(2,1)}, u32[]{:S(2)}) copy-start(bf16[128,128]{1,0:T(8,128)(2,1)} %wv_ref.1) | copy-start | bytes 98308
  4.4 0.8 %copy-start.4 = (bf16[128,128]{1,0:T(8,128)(2,1)S(1)}, bf16[128,128]{1,0:T(8,128)(2,1)}, u32[]{:S(2)}) copy-start(bf16[128,128]{1,0:T(8,128)(2,1)} %wg_ref.1) | copy-start | bytes 98308
  5.2 0.8 %copy-start.5 = (bf16[128,128]{1,0:T(8,128)(2,1)S(1)}, bf16[128,128]{1,0:T(8,128)(2,1)}, u32[]{:S(2)}) copy-start(bf16[128,128]{1,0:T(8,128)(2,1)} %wo_ref.1) | copy-start | bytes 98308

commit v2 on v1

--- a/solution.py
+++ b/solution.py
@@ -19,6 +19,16 @@
 
 
 def kernel(
+    pair_hbm,
+    gain_hbm,
+    wq_hbm,
+    wk_hbm,
+    wv_hbm,
+    wg_hbm,
+    bw_hbm,
+    wo_hbm,
+    upd_ref,
+    mir_ref,
     pair_ref,
     gain_ref,
     wq_ref,
@@ -27,8 +37,7 @@
     wg_ref,
     bw_ref,
     wo_ref,
-    upd_ref,
-    mir_ref,
+    in_sem,
     nrm,
     xcat,
     wbd,
@@ -45,6 +54,7 @@
     ufull,
     mstage,
     mflat,
+    mturn,
     s1_s,
     s1_r,
     s2_s,
@@ -105,6 +115,24 @@
 
         lax.fori_loop(low, high, step, 0)
 
+    loads = [
+        pltpu.make_async_copy(src, dst, in_sem.at[i])
+        for i, (src, dst) in enumerate(
+            (
+                (pair_hbm, pair_ref),
+                (gain_hbm, gain_ref),
+                (bw_hbm, bw_ref),
+                (wk_hbm, wk_ref),
+                (wv_hbm, wv_ref),
+                (wq_hbm, wq_ref),
+                (wg_hbm, wg_ref),
+                (wo_hbm, wo_ref),
+            )
+        )
+    ]
+    for load in loads:
+        load.start()
+
     barrier = pltpu.get_barrier_semaphore()
 
     def greet(dev):
@@ -115,6 +143,8 @@
     loop(1, 4, lambda k: greet((x_row((x + k) % 4), c)))
     greet(sibling)
 
+    loads[0].wait()
+    loads[1].wait()
     entries = pair_ref[...].reshape(512, 128).astype(jnp.float32)
     center = jnp.mean(entries, axis=-1, keepdims=True)
     shifted = entries - center
@@ -124,18 +154,22 @@
     nrm[...] = normed.reshape(16, 32, 128)
 
     xcat[...] = jnp.zeros_like(xcat)
-    place = pl.multiple_of((y % 4) * 32, 32)
     for j in range(16):
-        xcat[pl.ds(place, 32), j * 128 : (j + 1) * 128] = nrm[j]
+        xcat[0:32, j * 128 : (j + 1) * 128] = nrm[j]
     heads = lax.broadcasted_iota(jnp.int32, (64, 4), 0) // 16
     pick = heads == lax.broadcasted_iota(jnp.int32, (64, 4), 1)
-    spread_w = dot_nt(pick.astype(jnp.float32).astype(jnp.bfloat16), bw_ref[...])
+    loads[2].wait()
+    spread_w = dot(pick.astype(jnp.float32).astype(jnp.bfloat16), bw_ref[...])
     row_j = lax.broadcasted_iota(jnp.int32, (64, 128), 0) % 16
     for j in range(16):
         wbd[:, j * 128 : (j + 1) * 128] = jnp.where(row_j == j, spread_w, 0.0).astype(
             jnp.bfloat16
         )
-    b1buf[y] = dot_nt(wbd[...], xcat[...]).astype(jnp.bfloat16)
+    by_head = dot_nt(wbd[...], xcat[...])
+    packed = by_head[0:16]
+    for h in range(1, 4):
+        packed = packed + pltpu.roll(by_head[16 * h : 16 * h + 16], 32 * h, 1)
+    b1buf[y] = packed.astype(jnp.bfloat16)
 
     pl.semaphore_wait(barrier, 26)
 
@@ -159,11 +193,18 @@
     xall[0, pl.ds(own_slot, 32)] = nrm[c]
 
     loop(1, 8, lambda k: arrived(b1buf.at[0], b1_r.at[k]))
+    lane_group = lax.broadcasted_iota(jnp.int32, (16, 128), 1) // 32
     for g in range(2):
-        merged = b1buf[4 * g].astype(jnp.float32)
-        for i in range(1, 4):
-            merged = merged + b1buf[4 * g + i].astype(jnp.float32)
-        bbuf[core, z, :, g * 128 : (g + 1) * 128] = merged.astype(jnp.bfloat16)
+        tiles = [b1buf[4 * g + i].astype(jnp.float32) for i in range(4)]
+        for h in range(4):
+            merged = jnp.zeros((16, 128), jnp.float32)
+            for i in range(4):
+                turn = (i - h) * 32 % 128
+                moved = pltpu.roll(tiles[i], turn, 1) if turn else tiles[i]
+                merged = jnp.where(lane_group == i, moved, merged)
+            bbuf[core, z, h * 16 : (h + 1) * 16, g * 128 : (g + 1) * 128] = merged.astype(
+                jnp.bfloat16
+            )
     own_bias = bbuf.at[core, z]
     loop(1, 8, lambda k: send(own_bias, own_bias, b2_s.at[k], b2_r.at[k], z_peer(k)))
     send(own_bias, own_bias, b3_s.at[0], b3_r.at[0], sibling)
@@ -188,6 +229,8 @@
         qbuf[d] = (dot(own, wq_ref[...]) * 32**-0.5).astype(jnp.bfloat16)
         gbuf[d] = jax.nn.sigmoid(dot(own, wg_ref[...]))
 
+    for load in loads[3:]:
+        load.wait()
     project(0)
 
     def forward(k):
@@ -260,20 +303,33 @@
 
         loop(0, 8, one)
 
-    loop(0, 4, emit)
+    loop(0, 4, lambda n: emit((n + 1) % 4))
     ufull[x] = ustage[0]
 
-    loop(1, 4, lambda d: arrived(ufull.at[0], o1_r.at[d]))
-
-    def give(k):
-        cc = (c + k) % 16
-        rows = pl.ds(pl.multiple_of((cc % 4) * 32, 32), 32)
-        send(
-            ufull.at[cc // 4, rows], upd_ref.at[c], o2_s.at[k], o2_r.at[k], col_peer(k)
-        )
-
-    loop(1, 16, give)
-    upd_ref[c] = ufull[c // 4, pl.ds(pl.multiple_of((c % 4) * 32, 32), 32)]
+    def give(group):
+        def one(q):
+            cc = group * 4 + q
+            src = ufull.at[group, pl.ds(pl.multiple_of(q * 32, 32), 32)]
+            dst = upd_ref.at[c]
+            k = (cc - c + 16) % 16
+
+            @pl.when(cc == c)
+            def _():
+                pltpu.make_async_copy(src, dst, o2_r.at[0]).start()
+
+            @pl.when(cc != c)
+            def _():
+                send(src, dst, o2_s.at[k], o2_r.at[k], (r, cc))
+
+        loop(0, 4, one)
+
+    give(x)
+
+    def pass_on(d):
+        arrived(ufull.at[0], o1_r.at[d])
+        give((x + d) % 4)
+
+    loop(1, 4, pass_on)
 
     loop(1, 8, lambda k: arrived(b1buf.at[0], b1_s.at[k]))
     loop(1, 16, lambda k: arrived(nrm.at[0], s1_s.at[k]))
@@ -285,7 +341,9 @@
     loop(0, 32, lambda k: arrived(mstage.at[0], m_r.at[k]))
     mflat[...] = mstage[...].astype(jnp.float32).reshape(512, 128)
     for j in range(16):
-        mir_ref[j] = mflat[pl.ds(j, 32, stride=16), :].astype(jnp.bfloat16)
+        mturn[j] = mflat[pl.ds(j, 32, stride=16), :].astype(jnp.bfloat16)
+    own_mirror = pltpu.make_async_copy(mturn, mir_ref, o2_s.at[0])
+    own_mirror.start()
 
     def mirror_left(d):
         def one(t):
@@ -298,25 +356,53 @@
         loop(0, 8, one)
 
     loop(0, 4, mirror_left)
-    loop(1, 16, lambda k: arrived(upd_ref.at[0], o2_r.at[k]))
+    own_mirror.wait()
+    loop(0, 16, lambda k: arrived(upd_ref.at[0], o2_r.at[k]))
     loop(1, 16, lambda k: arrived(upd_ref.at[0], o2_s.at[k]))
+
+
+def place(upd_hbm, mir_hbm, upd_out, mir_out, upd, mir, sem):
+    reads = [
+        pltpu.make_async_copy(upd_hbm, upd, sem.at[0]),
+        pltpu.make_async_copy(mir_hbm, mir, sem.at[1]),
+    ]
+    writes = [
+        pltpu.make_async_copy(upd, upd_out, sem.at[0]),
+        pltpu.make_async_copy(mir, mir_out, sem.at[1]),
+    ]
+    for read in reads:
+        read.start()
+    for read, write in zip(reads, writes):
+        read.wait()
+        write.start()
+    for write in writes:
+        write.wait()
 
 
 def per_device(pair, gain, wq, wk, wv, wg, bw, wo):
     bf16, f32 = jnp.bfloat16, jnp.float32
-    vmem = pl.BlockSpec(memory_space=pltpu.VMEM)
+    hbm = pl.BlockSpec(memory_space=pl.ANY)
     dma = pltpu.SemaphoreType.DMA
     tile = jax.ShapeDtypeStruct(pair.shape, bf16)
-    return pl.pallas_call(
+    update, mirrored = pl.pallas_call(
         kernel,
         out_shape=(tile, tile),
-        in_specs=[vmem] * 8,
-        out_specs=(vmem, vmem),
+        in_specs=[hbm] * 8,
+        out_specs=(hbm, hbm),
         scratch_shapes=[
+            pltpu.VMEM((16, 32, 128), bf16),
+            pltpu.VMEM((1, 128), bf16),
+            pltpu.VMEM((128, 128), bf16),
+            pltpu.VMEM((128, 128), bf16),
+            pltpu.VMEM((128, 128), bf16),
+            pltpu.VMEM((128, 128), bf16),
+            pltpu.VMEM((4, 128), bf16),
+            pltpu.VMEM((128, 128), bf16),
+            dma((8,)),
             pltpu.VMEM((16, 32, 128), bf16),
             pltpu.VMEM((128, 2048), bf16),
             pltpu.VMEM((64, 2048), bf16),
-            pltpu.VMEM((8, 64, 128), bf16),
+            pltpu.VMEM((8, 16, 128), bf16),
             pltpu.VMEM((2, 8, 64, 256), bf16),
             pltpu.VMEM((4, 128, 512), f32),
             pltpu.VMEM((4, 512, 128), bf16),
@@ -329,6 +415,7 @@
             pltpu.VMEM((4, 128, 128), bf16),
             pltpu.VMEM((32, 16, 128), bf16),
             pltpu.VMEM((512, 128), f32),
+            pltpu.VMEM((16, 32, 128), bf16),
             dma((16,)),
             dma((16,)),
             dma((4,)),
@@ -347,12 +434,25 @@
             dma((32,)),
         ],
         compiler_params=pltpu.CompilerParams(
-            collective_id=0, has_side_effects=True, vmem_limit_bytes=48 * 2**20
+            collective_id=0, has_side_effects=True, vmem_limit_bytes=56 * 2**20
         ),
         cost_estimate=pl.CostEstimate(
             flops=1_000_000_000, bytes_accessed=1_000_000, transcendentals=1_100_000
         ),
-    )(pair, gain.reshape(1, 128), wq, wk, wv, wg, bw, wo)
+    )(pair, gain.reshape(1, 128), wq, wk, wv, wg, bw.T, wo)
+    return pl.pallas_call(
+        place,
+        out_shape=(tile, tile),
+        in_specs=[hbm, hbm],
+        out_specs=(hbm, hbm),
+        scratch_shapes=[
+            pltpu.VMEM((16, 32, 128), bf16),
+            pltpu.VMEM((16, 32, 128), bf16),
+            dma((2,)),
+        ],
+        compiler_params=pltpu.CompilerParams(vmem_limit_bytes=56 * 2**20),
+        cost_estimate=pl.CostEstimate(flops=0, bytes_accessed=524288, transcendentals=0),
+    )(update, mirrored)
 
 
 def solution(mesh):

time: 56.3 us -> 48.8 us (0.87)
  local copies, waits for them, and re-layouts: 6.57 us -> 0 us
  Pallas kernels: 48.6 us -> 48 us
    unnamed x19 -> x0, local copies, waits for them, and re-layouts: 6.57 us -> none
    pallas_call x1 -> x2, Pallas kernels: 48.6 us -> 48 us  [the longest x1 46.4 us: per_device(): pl.pallas_call(kernel, out_shape=(tile, tile), in_specs=[hbm] * 8, out_sp...]
where the time goes in v2:
time: 48.8 us; the launch traced here: 48.6 us
  Pallas kernels  48 us (98%)
  between operations  0.64 us (1%)
    pallas_call x1, Pallas kernels, per_device(): pl.pallas_call(kernel, out_shape=(tile, tile), in_specs=[hbm] * 8, out_sp...  46.4 us
    pallas_call x1, Pallas kernels, per_device(): pl.pallas_call(place, out_shape=(tile, tile), in_specs=[hbm, hbm], out_sp...  1.64 us

profile of v2, /device:TPU:1, one launch (start us, length us, event | category | flops | bytes accessed | tf_op | source)
XLA Modules:
  0.0 48.6 jit_solution(6304158771156425386)
XLA Ops:
  0.6 46.4 %shard_map.95 = (bf16[16,32,128]{2,1,0:T(8,128)(2,1)}, bf16[16,32,128]{2,1,0:T(8,128)(2,1)}) custom-call(bf16[16,32,128]{2,1,0:T(8,128)(2,1)} %pair_hbm.1, bf16[1,128]{1,0:T(2,128)(2,1)} %bitcast.3, bf16[128,128]{1,0:T(8,128)(2,1)} %wq_hbm.1, bf16[128,128]{1,0:T(8,128)(2,1)} %wk_hbm.1, bf16[128,128]{1,0:T(8,128)(2,1)} %wv_hbm.1, bf16[128,128]{1,0:T(8,128)(2,1)} %wg_hbm.1, ...), custom_call_target="tpu_custom_call" | custom-call | flops 1000000000 | bytes 1000000 | tf_op jit(solution)/shard_map/pallas_call | solution.py:387
  47.0 1.6 %shard_map.96 = (bf16[16,32,128]{2,1,0:T(8,128)(2,1)}, bf16[16,32,128]{2,1,0:T(8,128)(2,1)}) custom-call(bf16[16,32,128]{2,1,0:T(8,128)(2,1)} %get-tuple-element.4.upd_hbm, bf16[16,32,128]{2,1,0:T(8,128)(2,1)} %get-tuple-element.5.mir_hbm), custom_call_target="tpu_custom_call" | custom-call | bytes 524288 | tf_op jit(solution)/shard_map/pallas_call | solution.py:443

commit v3 on v2

--- a/solution.py
+++ b/solution.py
@@ -12,6 +12,18 @@
 
 def dot(a, b):
     return jnp.dot(a, b, preferred_element_type=jnp.float32)
+
+
+def div(a, b):
+    return lax.div(a, jnp.int32(b))
+
+
+def rem(a, b):
+    return lax.rem(a, jnp.int32(b))
+
+
+def outward(n, middle):
+    return middle + div(n + 1, 2) * (1 - 2 * rem(n, 2))
 
 
 def dot_nt(a, b):
@@ -45,9 +57,11 @@
     bbuf,
     biasf,
     xall,
-    kbuf,
+    wkt,
     vbuf,
-    qbuf,
+    scores,
+    weights,
+    inverse,
     gbuf,
     xq,
     ustage,
@@ -74,26 +88,26 @@
 ):
     r = lax.axis_index("row")
     c = lax.axis_index("col")
-    x = r // 8
-    zh = (r // 2) % 4
-    core = r % 2
-    y = c // 2
-    zl = c % 2
+    x = div(r, 8)
+    zh = rem(div(r, 2), 4)
+    core = rem(r, 2)
+    y = div(c, 2)
+    zl = rem(c, 2)
     z = zh * 2 + zl
     sibling = (r + 1 - 2 * core, c)
 
     def col_peer(k):
-        return (r, (c + k) % 16)
+        return (r, rem(c + k, 16))
 
     def x_row(xx):
         return xx * 8 + zh * 2 + core
 
     def y_peer(k):
-        return (r, ((y + k) % 8) * 2 + zl)
+        return (r, rem(y + k, 8) * 2 + zl)
 
     def z_peer(k):
-        zz = (z + k) % 8
-        return (x * 8 + (zz // 2) * 2 + core, y * 2 + zz % 2)
+        zz = rem(z + k, 8)
+        return (x * 8 + div(zz, 2) * 2 + core, y * 2 + rem(zz, 2))
 
     def send(src, dst, s_sem, r_sem, dev):
         pltpu.make_async_remote_copy(
@@ -130,18 +144,19 @@
             )
         )
     ]
-    for load in loads:
-        load.start()
+    loads[0].start()
 
     barrier = pltpu.get_barrier_semaphore()
 
     def greet(dev):
         pl.semaphore_signal(barrier, inc=1, device_id=dev, device_id_type=MESH)
 
-    loop(1, 16, lambda k: greet(col_peer(k)))
-    loop(1, 8, lambda k: greet(z_peer(k)))
-    loop(1, 4, lambda k: greet((x_row((x + k) % 4), c)))
+    loop(0, 15, lambda n: greet(col_peer(outward(n, 8))))
+    loop(0, 7, lambda n: greet(z_peer(outward(n, 4))))
+    loop(1, 4, lambda k: greet((x_row(rem(x + k, 4)), c)))
     greet(sibling)
+    for load in loads[1:]:
+        load.start()
 
     loads[0].wait()
     loads[1].wait()
@@ -171,25 +186,29 @@
         packed = packed + pltpu.roll(by_head[16 * h : 16 * h + 16], 32 * h, 1)
     b1buf[y] = packed.astype(jnp.bfloat16)
 
+    loads[3].wait()
+    wkt[...] = wk_ref[...].astype(jnp.float32).T.astype(jnp.bfloat16)
+
     pl.semaphore_wait(barrier, 26)
 
-    loop(
-        1,
-        8,
-        lambda k: send(b1buf.at[y], b1buf.at[y], b1_s.at[k], b1_r.at[k], y_peer(k)),
-    )
+    def send_tile(n):
+        k = outward(n, 4)
+        send(b1buf.at[y], b1buf.at[y], b1_s.at[k], b1_r.at[k], y_peer(k))
+
+    loop(0, 7, send_tile)
     own_slot = pl.multiple_of((zl * 8 + y) * 32, 32)
-    loop(
-        1,
-        16,
-        lambda k: send(
-            nrm.at[(c + k) % 16],
+
+    def send_row(n):
+        k = outward(n, 8)
+        send(
+            nrm.at[rem(c + k, 16)],
             xall.at[0, pl.ds(own_slot, 32)],
             s1_s.at[k],
             s1_r.at[k],
             col_peer(k),
-        ),
-    )
+        )
+
+    loop(0, 15, send_row)
     xall[0, pl.ds(own_slot, 32)] = nrm[c]
 
     loop(1, 8, lambda k: arrived(b1buf.at[0], b1_r.at[k]))
@@ -206,7 +225,12 @@
                 jnp.bfloat16
             )
     own_bias = bbuf.at[core, z]
-    loop(1, 8, lambda k: send(own_bias, own_bias, b2_s.at[k], b2_r.at[k], z_peer(k)))
+
+    def send_bias(n):
+        k = outward(n, 4)
+        send(own_bias, own_bias, b2_s.at[k], b2_r.at[k], z_peer(k))
+
+    loop(0, 7, send_bias)
     send(own_bias, own_bias, b3_s.at[0], b3_r.at[0], sibling)
 
     loop(1, 16, lambda k: arrived(xall.at[0, pl.ds(0, 32)], s1_r.at[k]))
@@ -214,32 +238,54 @@
         1,
         4,
         lambda d: send(
-            xall.at[0], xall.at[d], s2_s.at[d], s2_r.at[d], (x_row((x + d) % 4), c)
+            xall.at[0], xall.at[d], s2_s.at[d], s2_r.at[d], (x_row(rem(x + d, 4)), c)
         ),
     )
 
     def project(d):
         keys = xall[d]
-        kbuf[d] = dot(keys, wk_ref[...]).astype(jnp.bfloat16)
-        vbuf[d] = dot(keys, wv_ref[...]).astype(jnp.bfloat16)
+        kt = dot_nt(wkt[...], keys).astype(jnp.bfloat16)
+        values = dot(keys, wv_ref[...])
+        for h in range(4):
+            vbuf[d, h * 512 : (h + 1) * 512] = jnp.where(
+                head_of_key == h, values, 0.0
+            ).astype(jnp.bfloat16)
         for q in range(4):
             slot = pl.multiple_of(((q % 2) * 8 + 2 * x + q // 2) * 32, 32)
             xq[q * 32 : (q + 1) * 32] = xall[d, pl.ds(slot, 32)]
         own = xq[...]
-        qbuf[d] = (dot(own, wq_ref[...]) * 32**-0.5).astype(jnp.bfloat16)
         gbuf[d] = jax.nn.sigmoid(dot(own, wg_ref[...]))
-
-    for load in loads[3:]:
+        queries = (dot(own, wq_ref[...]) * 32**-0.5).astype(jnp.bfloat16)
+        queries = queries.astype(jnp.float32)
+        by_head = [
+            jnp.where(head_of_lane == h, queries, 0.0).astype(jnp.bfloat16)
+            for h in range(4)
+        ]
+        scores[d] = dot(jnp.concatenate(by_head, 0), kt)
+
+    def lay_bias(half, zz):
+        block = bbuf[half, zz].astype(jnp.float32)
+        j0 = pl.multiple_of((div(zz, 2) * 2 + half) * 16, 16)
+        for h in range(4):
+            biasf[rem(zz, 2), h, pl.ds(j0, 16)] = block[h * 16 : (h + 1) * 16]
+
+    head_of_lane = lax.broadcasted_iota(jnp.int32, (128, 128), 1) // 32
+    head_of_key = lax.broadcasted_iota(jnp.int32, (512, 128), 1) // 32
+
+    for load in loads[4:]:
         load.wait()
     project(0)
-
-    def forward(k):
-        zz = (z - k + 8) % 8
+    lay_bias(core, z)
+
+    def forward(n):
+        k = outward(6 - n, 4)
+        zz = rem(z - k + 8, 8)
         block = bbuf.at[core, zz]
         arrived(block, b2_r.at[k])
         send(block, block, b3_s.at[k], b3_r.at[k], sibling)
-
-    loop(1, 8, forward)
+        lay_bias(core, zz)
+
+    loop(0, 7, forward)
 
     def next_row(d):
         arrived(xall.at[d], s2_r.at[d])
@@ -247,32 +293,32 @@
 
     loop(1, 4, next_row)
 
-    loop(0, 8, lambda k: arrived(bbuf.at[0, 0], b3_r.at[k]))
-    for half in range(2):
-        for zz in range(8):
-            j0 = ((zz // 2) * 2 + half) * 16
-            k0 = (zz % 2) * 256
-            block = bbuf[half, zz].astype(jnp.float32)
-            for h in range(4):
-                biasf[h, j0 : j0 + 16, k0 : k0 + 256] = block[h * 16 : (h + 1) * 16]
-
-    head_of_lane = lax.broadcasted_iota(jnp.int32, (128, 128), 1) // 32
-
-    def attend(d):
-        queries = qbuf[d].astype(jnp.float32)
-        attended = jnp.zeros((128, 128), jnp.float32)
+    def take_bias(n):
+        k = outward(7 - n, 4)
+        zz = rem(z - k + 8, 8)
+        arrived(bbuf.at[0, 0], b3_r.at[k])
+        lay_bias(1 - core, zz)
+
+    loop(0, 8, take_bias)
+
+    def weigh(d):
+        scale = jnp.zeros((128, 128), jnp.float32)
         for h in range(4):
-            mine = jnp.where(head_of_lane == h, queries, 0.0).astype(jnp.bfloat16)
-            scores = dot_nt(mine, kbuf[d]) + biasf[h]
-            exponent = jnp.exp(scores - jnp.max(scores, axis=-1, keepdims=True))
+            bias = jnp.concatenate([biasf[0, h], biasf[1, h]], 1)
+            logits = scores[d, h * 128 : (h + 1) * 128] + bias
+            exponent = jnp.exp(logits - jnp.max(logits, axis=-1, keepdims=True))
             denominator = jnp.sum(exponent, axis=-1, keepdims=True)
-            mixed = dot(exponent.astype(jnp.bfloat16), vbuf[d])
-            attended = jnp.where(head_of_lane == h, mixed / denominator, attended)
+            weights[d, :, h * 512 : (h + 1) * 512] = exponent.astype(jnp.bfloat16)
+            scale = jnp.where(head_of_lane == h, 1.0 / denominator, scale)
+        inverse[d] = scale
+
+    def mix(d):
+        attended = dot(weights[d], vbuf[d]) * inverse[d]
         gated = (gbuf[d] * attended).astype(jnp.bfloat16)
         ustage[d] = dot(gated, wo_ref[...]).astype(jnp.bfloat16)
 
     def mirror_copy(d, t):
-        x_i = (x - d + 4) % 4
+        x_i = rem(x - d + 4, 4)
         to_row = x * 8 + t
         to_col = x_i * 4 + zh
         src = ustage.at[d, pl.ds(pl.multiple_of(t * 16, 16), 16)]
@@ -283,14 +329,12 @@
         return src, dst, s_sem, r_sem, (to_row, to_col), here
 
     def emit(d):
-        attend(d)
-        x_i = (x - d + 4) % 4
-
-        @pl.when(d > 0)
-        def _():
-            send(ustage.at[d], ufull.at[x], o1_s.at[d], o1_r.at[d], (x_row(x_i), c))
-
-        def one(t):
+        if d > 0:
+            dev = (x_row(rem(x - d + 4, 4)), c)
+            send(ustage.at[d], ufull.at[x], o1_s.at[d], o1_r.at[d], dev)
+
+        def one(n):
+            t = rem(zh * 2 + 4 + n, 8)
             src, dst, s_sem, r_sem, dev, here = mirror_copy(d, t)
 
             @pl.when(here)
@@ -303,7 +347,18 @@
 
         loop(0, 8, one)
 
-    loop(0, 4, lambda n: emit((n + 1) % 4))
+    weigh(1)
+    weigh(2)
+    mix(1)
+    emit(1)
+    weigh(3)
+    mix(2)
+    emit(2)
+    weigh(0)
+    mix(3)
+    emit(3)
+    mix(0)
+    emit(0)
     ufull[x] = ustage[0]
 
     def give(group):
@@ -311,7 +366,7 @@
             cc = group * 4 + q
             src = ufull.at[group, pl.ds(pl.multiple_of(q * 32, 32), 32)]
             dst = upd_ref.at[c]
-            k = (cc - c + 16) % 16
+            k = rem(cc - c + 16, 16)
 
             @pl.when(cc == c)
             def _():
@@ -327,7 +382,7 @@
 
     def pass_on(d):
         arrived(ufull.at[0], o1_r.at[d])
-        give((x + d) % 4)
+        give(rem(x + d, 4))
 
     loop(1, 4, pass_on)
 
@@ -404,11 +459,13 @@
             pltpu.VMEM((64, 2048), bf16),
             pltpu.VMEM((8, 16, 128), bf16),
             pltpu.VMEM((2, 8, 64, 256), bf16),
-            pltpu.VMEM((4, 128, 512), f32),
+            pltpu.VMEM((2, 4, 128, 256), f32),
             pltpu.VMEM((4, 512, 128), bf16),
-            pltpu.VMEM((4, 512, 128), bf16),
-            pltpu.VMEM((4, 512, 128), bf16),
-            pltpu.VMEM((4, 128, 128), bf16),
+            pltpu.VMEM((128, 128), bf16),
+            pltpu.VMEM((4, 2048, 128), bf16),
+            pltpu.VMEM((4, 512, 512), f32),
+            pltpu.VMEM((4, 128, 2048), bf16),
+            pltpu.VMEM((4, 128, 128), f32),
             pltpu.VMEM((4, 128, 128), f32),
             pltpu.VMEM((128, 128), bf16),
             pltpu.VMEM((4, 128, 128), bf16),

time: 48.8 us -> 44.9 us (0.920)
  Pallas kernels: 48 us -> 43.7 us
    pallas_call x1, Pallas kernels: 46.4 us -> 42.1 us  [per_device(): pl.pallas_call(kernel, out_shape=(tile, tile), in_specs=[hbm] * 8, out_sp...]
where the time goes in v3:
time: 44.9 us; the launch traced here: 44.4 us
  Pallas kernels  43.7 us (97%)
  between operations  0.64 us (1%)
    pallas_call x1, Pallas kernels, per_device(): pl.pallas_call(kernel, out_shape=(tile, tile), in_specs=[hbm] * 8, out_sp...  42.1 us
    pallas_call x1, Pallas kernels, per_device(): pl.pallas_call(place, out_shape=(tile, tile), in_specs=[hbm, hbm], out_sp...  1.64 us

profile of v3, /device:TPU:1, one launch (start us, length us, event | category | flops | bytes accessed | tf_op | source)
XLA Modules:
  0.0 44.4 jit_solution(885533324256342688)
XLA Ops:
  0.6 42.1 %shard_map.95 = (bf16[16,32,128]{2,1,0:T(8,128)(2,1)}, bf16[16,32,128]{2,1,0:T(8,128)(2,1)}) custom-call(bf16[16,32,128]{2,1,0:T(8,128)(2,1)} %pair_hbm.1, bf16[1,128]{1,0:T(2,128)(2,1)} %bitcast.3, bf16[128,128]{1,0:T(8,128)(2,1)} %wq_hbm.1, bf16[128,128]{1,0:T(8,128)(2,1)} %wk_hbm.1, bf16[128,128]{1,0:T(8,128)(2,1)} %wv_hbm.1, bf16[128,128]{1,0:T(8,128)(2,1)} %wg_hbm.1, ...), custom_call_target="tpu_custom_call" | custom-call | flops 1000000000 | bytes 1000000 | tf_op jit(solution)/shard_map/pallas_call | solution.py:442
  42.7 1.6 %shard_map.96 = (bf16[16,32,128]{2,1,0:T(8,128)(2,1)}, bf16[16,32,128]{2,1,0:T(8,128)(2,1)}) custom-call(bf16[16,32,128]{2,1,0:T(8,128)(2,1)} %get-tuple-element.4.upd_hbm, bf16[16,32,128]{2,1,0:T(8,128)(2,1)} %get-tuple-element.5.mir_hbm), custom_call_target="tpu_custom_call" | custom-call | bytes 524288 | tf_op jit(solution)/shard_map/pallas_call | solution.py:500

commit v4 on v3

--- a/solution.py
+++ b/solution.py
@@ -7,6 +7,7 @@
 
 EPSILON = 1e-05
 MESH = pl.DeviceIdType.MESH
+EARLY = 6
 NT = (((1,), (1,)), ((), ()))
 
 
@@ -68,7 +69,6 @@
     ufull,
     mstage,
     mflat,
-    mturn,
     s1_s,
     s1_r,
     s2_s,
@@ -144,7 +144,8 @@
             )
         )
     ]
-    loads[0].start()
+    for load in loads[:3]:
+        load.start()
 
     barrier = pltpu.get_barrier_semaphore()
 
@@ -155,11 +156,22 @@
     loop(0, 7, lambda n: greet(z_peer(outward(n, 4))))
     loop(1, 4, lambda k: greet((x_row(rem(x + k, 4)), c)))
     greet(sibling)
-    for load in loads[1:]:
+    for load in loads[3:]:
         load.start()
 
+    xcat[32:128] = jnp.zeros((96, 2048), jnp.bfloat16)
+    heads = lax.broadcasted_iota(jnp.int32, (64, 4), 0) // 16
+    pick = heads == lax.broadcasted_iota(jnp.int32, (64, 4), 1)
+    row_j = lax.broadcasted_iota(jnp.int32, (64, 128), 0) % 16
+    loads[2].wait()
+    spread_w = dot(pick.astype(jnp.float32).astype(jnp.bfloat16), bw_ref[...])
+    for j in range(16):
+        wbd[:, j * 128 : (j + 1) * 128] = jnp.where(row_j == j, spread_w, 0.0).astype(
+            jnp.bfloat16
+        )
+
+    loads[1].wait()
     loads[0].wait()
-    loads[1].wait()
     entries = pair_ref[...].reshape(512, 128).astype(jnp.float32)
     center = jnp.mean(entries, axis=-1, keepdims=True)
     shifted = entries - center
@@ -168,32 +180,19 @@
     normed = (shifted * lax.rsqrt(spread + EPSILON) * gain).astype(jnp.bfloat16)
     nrm[...] = normed.reshape(16, 32, 128)
 
-    xcat[...] = jnp.zeros_like(xcat)
     for j in range(16):
         xcat[0:32, j * 128 : (j + 1) * 128] = nrm[j]
-    heads = lax.broadcasted_iota(jnp.int32, (64, 4), 0) // 16
-    pick = heads == lax.broadcasted_iota(jnp.int32, (64, 4), 1)
-    loads[2].wait()
-    spread_w = dot(pick.astype(jnp.float32).astype(jnp.bfloat16), bw_ref[...])
-    row_j = lax.broadcasted_iota(jnp.int32, (64, 128), 0) % 16
-    for j in range(16):
-        wbd[:, j * 128 : (j + 1) * 128] = jnp.where(row_j == j, spread_w, 0.0).astype(
-            jnp.bfloat16
-        )
     by_head = dot_nt(wbd[...], xcat[...])
     packed = by_head[0:16]
     for h in range(1, 4):
         packed = packed + pltpu.roll(by_head[16 * h : 16 * h + 16], 32 * h, 1)
     b1buf[y] = packed.astype(jnp.bfloat16)
 
-    loads[3].wait()
-    wkt[...] = wk_ref[...].astype(jnp.float32).T.astype(jnp.bfloat16)
-
     pl.semaphore_wait(barrier, 26)
 
     def send_tile(n):
         k = outward(n, 4)
-        send(b1buf.at[y], b1buf.at[y], b1_s.at[k], b1_r.at[k], y_peer(k))
+        send(b1buf.at[y], b1buf.at[y], b1_s, b1_r, y_peer(k))
 
     loop(0, 7, send_tile)
     own_slot = pl.multiple_of((zl * 8 + y) * 32, 32)
@@ -203,7 +202,7 @@
         send(
             nrm.at[rem(c + k, 16)],
             xall.at[0, pl.ds(own_slot, 32)],
-            s1_s.at[k],
+            s1_s,
             s1_r.at[k],
             col_peer(k),
         )
@@ -211,7 +210,22 @@
     loop(0, 15, send_row)
     xall[0, pl.ds(own_slot, 32)] = nrm[c]
 
-    loop(1, 8, lambda k: arrived(b1buf.at[0], b1_r.at[k]))
+    def share(col):
+        rows = pl.ds(pl.multiple_of((rem(col, 2) * 8 + div(col, 2)) * 32, 32), 32)
+        piece = xall.at[0, rows]
+        for d in (2, 1, 3):
+            dev = (x_row(rem(x + d, 4)), c)
+            send(piece, xall.at[d, rows], s2_s.at[d], s2_r.at[d], dev)
+
+    def pass_row(n):
+        k = outward(14 - n, 8)
+        arrived(xall.at[0, pl.ds(0, 32)], s1_r.at[k])
+        share(rem(c - k + 16, 16))
+
+    share(c)
+    loop(0, EARLY, pass_row)
+
+    arrived(b1buf.at[pl.ds(0, 7)], b1_r)
     lane_group = lax.broadcasted_iota(jnp.int32, (16, 128), 1) // 32
     for g in range(2):
         tiles = [b1buf[4 * g + i].astype(jnp.float32) for i in range(4)]
@@ -233,14 +247,9 @@
     loop(0, 7, send_bias)
     send(own_bias, own_bias, b3_s.at[0], b3_r.at[0], sibling)
 
-    loop(1, 16, lambda k: arrived(xall.at[0, pl.ds(0, 32)], s1_r.at[k]))
-    loop(
-        1,
-        4,
-        lambda d: send(
-            xall.at[0], xall.at[d], s2_s.at[d], s2_r.at[d], (x_row(rem(x + d, 4)), c)
-        ),
-    )
+    loop(EARLY, 15, pass_row)
+    loads[3].wait()
+    wkt[...] = wk_ref[...].astype(jnp.float32).T.astype(jnp.bfloat16)
 
     def project(d):
         keys = xall[d]
@@ -291,7 +300,9 @@
         arrived(xall.at[d], s2_r.at[d])
         project(d)
 
-    loop(1, 4, next_row)
+    next_row(1)
+    next_row(3)
+    next_row(2)
 
     def take_bias(n):
         k = outward(7 - n, 4)
@@ -323,10 +334,8 @@
         to_col = x_i * 4 + zh
         src = ustage.at[d, pl.ds(pl.multiple_of(t * 16, 16), 16)]
         dst = mstage.at[core * 16 + c]
-        r_sem = m_r.at[core * 16 + c]
         here = jnp.logical_and(to_row == r, to_col == c)
-        s_sem = m_s.at[d * 8 + t]
-        return src, dst, s_sem, r_sem, (to_row, to_col), here
+        return src, dst, (to_row, to_col), here
 
     def emit(d):
         if d > 0:
@@ -335,25 +344,25 @@
 
         def one(n):
             t = rem(zh * 2 + 4 + n, 8)
-            src, dst, s_sem, r_sem, dev, here = mirror_copy(d, t)
+            src, dst, dev, here = mirror_copy(d, t)
 
             @pl.when(here)
             def _():
-                pltpu.make_async_copy(src, dst, r_sem).start()
+                pltpu.make_async_copy(src, dst, m_r).start()
 
             @pl.when(jnp.logical_not(here))
             def _():
-                send(src, dst, s_sem, r_sem, dev)
+                send(src, dst, m_s, m_r, dev)
 
         loop(0, 8, one)
 
+    weigh(2)
     weigh(1)
-    weigh(2)
+    mix(2)
+    emit(2)
+    weigh(3)
     mix(1)
     emit(1)
-    weigh(3)
-    mix(2)
-    emit(2)
     weigh(0)
     mix(3)
     emit(3)
@@ -366,15 +375,14 @@
             cc = group * 4 + q
             src = ufull.at[group, pl.ds(pl.multiple_of(q * 32, 32), 32)]
             dst = upd_ref.at[c]
-            k = rem(cc - c + 16, 16)
 
             @pl.when(cc == c)
             def _():
-                pltpu.make_async_copy(src, dst, o2_r.at[0]).start()
+                pltpu.make_async_copy(src, dst, o2_r).start()
 
             @pl.when(cc != c)
             def _():
-                send(src, dst, o2_s.at[k], o2_r.at[k], (r, cc))
+                send(src, dst, o2_s, o2_r, (r, cc))
 
         loop(0, 4, one)
 
@@ -384,51 +392,42 @@
         arrived(ufull.at[0], o1_r.at[d])
         give(rem(x + d, 4))
 
-    loop(1, 4, pass_on)
-
-    loop(1, 8, lambda k: arrived(b1buf.at[0], b1_s.at[k]))
-    loop(1, 16, lambda k: arrived(nrm.at[0], s1_s.at[k]))
+    pass_on(2)
+    pass_on(1)
+    pass_on(3)
+
+    arrived(b1buf.at[pl.ds(0, 7)], b1_s)
+    arrived(nrm.at[pl.ds(0, 15)], s1_s)
     loop(1, 8, lambda k: arrived(bbuf.at[0, 0], b2_s.at[k]))
     loop(0, 8, lambda k: arrived(bbuf.at[0, 0], b3_s.at[k]))
     loop(1, 4, lambda d: arrived(xall.at[0], s2_s.at[d]))
     loop(1, 4, lambda d: arrived(ustage.at[0], o1_s.at[d]))
 
-    loop(0, 32, lambda k: arrived(mstage.at[0], m_r.at[k]))
+    arrived(mstage, m_r)
     mflat[...] = mstage[...].astype(jnp.float32).reshape(512, 128)
     for j in range(16):
-        mturn[j] = mflat[pl.ds(j, 32, stride=16), :].astype(jnp.bfloat16)
-    own_mirror = pltpu.make_async_copy(mturn, mir_ref, o2_s.at[0])
-    own_mirror.start()
-
-    def mirror_left(d):
-        def one(t):
-            src, dst, s_sem, r_sem, dev, here = mirror_copy(d, t)
-
-            @pl.when(jnp.logical_not(here))
-            def _():
-                arrived(src, s_sem)
-
-        loop(0, 8, one)
-
-    loop(0, 4, mirror_left)
-    own_mirror.wait()
-    loop(0, 16, lambda k: arrived(upd_ref.at[0], o2_r.at[k]))
-    loop(1, 16, lambda k: arrived(upd_ref.at[0], o2_s.at[k]))
-
-
-def place(upd_hbm, mir_hbm, upd_out, mir_out, upd, mir, sem):
-    reads = [
-        pltpu.make_async_copy(upd_hbm, upd, sem.at[0]),
-        pltpu.make_async_copy(mir_hbm, mir, sem.at[1]),
-    ]
+        mir_ref[j] = mflat[pl.ds(j, 32, stride=16), :].astype(jnp.bfloat16)
+
+    stays = rem(c, 4) == zh
+
+    @pl.when(stays)
+    def _():
+        arrived(mstage.at[pl.ds(0, 31)], m_s)
+
+    @pl.when(jnp.logical_not(stays))
+    def _():
+        arrived(mstage, m_s)
+
+    arrived(upd_ref.at[pl.ds(0, 15)], o2_s)
+    arrived(upd_ref, o2_r)
+
+
+def place(upd, mir, upd_out, mir_out, sem):
     writes = [
         pltpu.make_async_copy(upd, upd_out, sem.at[0]),
         pltpu.make_async_copy(mir, mir_out, sem.at[1]),
     ]
-    for read in reads:
-        read.start()
-    for read, write in zip(reads, writes):
-        read.wait()
+    for write in writes:
         write.start()
     for write in writes:
         write.wait()
@@ -437,13 +436,19 @@
 def per_device(pair, gain, wq, wk, wv, wg, bw, wo):
     bf16, f32 = jnp.bfloat16, jnp.float32
     hbm = pl.BlockSpec(memory_space=pl.ANY)
+    vmem = pl.BlockSpec(memory_space=pltpu.VMEM)
+    near = pltpu.VMEM(pair.shape, bf16)
     dma = pltpu.SemaphoreType.DMA
     tile = jax.ShapeDtypeStruct(pair.shape, bf16)
+    far = [
+        pltpu.with_memory_space_constraint(array, pltpu.HBM)
+        for array in (pair, gain.reshape(1, 128), wq, wk, wv, wg, bw.T, wo)
+    ]
     update, mirrored = pl.pallas_call(
         kernel,
-        out_shape=(tile, tile),
+        out_shape=(near, near),
         in_specs=[hbm] * 8,
-        out_specs=(hbm, hbm),
+        out_specs=(vmem, vmem),
         scratch_shapes=[
             pltpu.VMEM((16, 32, 128), bf16),
             pltpu.VMEM((1, 128), bf16),
@@ -472,42 +477,37 @@
             pltpu.VMEM((4, 128, 128), bf16),
             pltpu.VMEM((32, 16, 128), bf16),
             pltpu.VMEM((512, 128), f32),
-            pltpu.VMEM((16, 32, 128), bf16),
-            dma((16,)),
+            dma,
             dma((16,)),
             dma((4,)),
             dma((4,)),
-            dma((8,)),
-            dma((8,)),
+            dma,
+            dma,
             dma((8,)),
             dma((8,)),
             dma((8,)),
             dma((8,)),
             dma((4,)),
             dma((4,)),
-            dma((16,)),
-            dma((16,)),
-            dma((32,)),
-            dma((32,)),
+            dma,
+            dma,
+            dma,
+            dma,
         ],
         compiler_params=pltpu.CompilerParams(
-            collective_id=0, has_side_effects=True, vmem_limit_bytes=56 * 2**20
+            collective_id=0, has_side_effects=True, vmem_limit_bytes=32 * 2**20
         ),
         cost_estimate=pl.CostEstimate(
             flops=1_000_000_000, bytes_accessed=1_000_000, transcendentals=1_100_000
         ),
-    )(pair, gain.reshape(1, 128), wq, wk, wv, wg, bw.T, wo)
+    )(*far)
     return pl.pallas_call(
         place,
         out_shape=(tile, tile),
-        in_specs=[hbm, hbm],
+        in_specs=[vmem, vmem],
         out_specs=(hbm, hbm),
-        scratch_shapes=[
-            pltpu.VMEM((16, 32, 128), bf16),
-            pltpu.VMEM((16, 32, 128), bf16),
-            dma((2,)),
-        ],
-        compiler_params=pltpu.CompilerParams(vmem_limit_bytes=56 * 2**20),
+        scratch_shapes=[dma((2,))],
+        compiler_params=pltpu.CompilerParams(vmem_limit_bytes=4 * 2**20),
         cost_estimate=pl.CostEstimate(flops=0, bytes_accessed=524288, transcendentals=0),
     )(update, mirrored)
 

time: 44.9 us -> 43.3 us (0.964)
  Pallas kernels: 43.7 us -> 42.4 us
    pallas_call x2, Pallas kernels: 43.7 us -> 42.4 us  [the longest x1 41.7 us: per_device(): pl.pallas_call(kernel, out_shape=(near, near), in_specs=[hbm] * 8, out_sp...]
where the time goes in v4:
time: 43.3 us; the launch traced here: 43 us
  Pallas kernels  42.4 us (98%)
  between operations  0.64 us (1%)
    pallas_call x1, Pallas kernels, per_device(): pl.pallas_call(kernel, out_shape=(near, near), in_specs=[hbm] * 8, out_sp...  41.7 us

profile of v4, /device:TPU:1, one launch (start us, length us, event | category | flops | bytes accessed | tf_op | source)
XLA Modules:
  0.0 43.0 jit_solution(9296955972589454356)
XLA Ops:
  0.6 41.7 %shard_map.95 = (bf16[16,32,128]{2,1,0:T(8,128)(2,1)S(1)}, bf16[16,32,128]{2,1,0:T(8,128)(2,1)S(1)}) custom-call(bf16[16,32,128]{2,1,0:T(8,128)(2,1)} %pair_hbm.1, bf16[1,128]{1,0:T(2,128)(2,1)} %bitcast.3, bf16[128,128]{1,0:T(8,128)(2,1)} %wq_hbm.1, bf16[128,128]{1,0:T(8,128)(2,1)} %wk_hbm.1, bf16[128,128]{1,0:T(8,128)(2,1)} %wv_hbm.1, ...), custom_call_target="tpu_custom_call" | custom-call | flops 1000000000 | bytes 1000000 | tf_op jit(solution)/shard_map/pallas_call | solution.py:447
  42.3 0.7 %shard_map.96 = (bf16[16,32,128]{2,1,0:T(8,128)(2,1)}, bf16[16,32,128]{2,1,0:T(8,128)(2,1)}) custom-call(bf16[16,32,128]{2,1,0:T(8,128)(2,1)S(1)} %get-tuple-element.4.upd, bf16[16,32,128]{2,1,0:T(8,128)(2,1)S(1)} %get-tuple-element.5.mir), custom_call_target="tpu_custom_call" | custom-call | bytes 524288 | tf_op jit(solution)/shard_map/pallas_call | solution.py:504

commit v5 on v4

--- a/solution.py
+++ b/solution.py
@@ -25,6 +25,11 @@
 
 def outward(n, middle):
     return middle + div(n + 1, 2) * (1 - 2 * rem(n, 2))
+
+
+def position(k):
+    below = 1 - div(k, 4)
+    return (1 - 2 * below) * 2 * (k - 4) - below
 
 
 def dot_nt(a, b):
@@ -186,32 +191,34 @@
     packed = by_head[0:16]
     for h in range(1, 4):
         packed = packed + pltpu.roll(by_head[16 * h : 16 * h + 16], 32 * h, 1)
-    b1buf[y] = packed.astype(jnp.bfloat16)
+    b1buf[7] = packed.astype(jnp.bfloat16)
 
     pl.semaphore_wait(barrier, 26)
 
     def send_tile(n):
         k = outward(n, 4)
-        send(b1buf.at[y], b1buf.at[y], b1_s, b1_r, y_peer(k))
+        send(b1buf.at[7], b1buf.at[n], b1_s, b1_r.at[n], y_peer(k))
 
     loop(0, 7, send_tile)
-    own_slot = pl.multiple_of((zl * 8 + y) * 32, 32)
+    def slot_rows(z_low, k):
+        return pl.ds(pl.multiple_of((z_low * 8 + position(k)) * 32, 32), 32)
 
     def send_row(n):
         k = outward(n, 8)
+        col = rem(c + k, 16)
         send(
-            nrm.at[rem(c + k, 16)],
-            xall.at[0, pl.ds(own_slot, 32)],
+            nrm.at[col],
+            xall.at[0, slot_rows(zl, rem(div(col, 2) - y + 8, 8))],
             s1_s,
             s1_r.at[k],
-            col_peer(k),
+            (r, col),
         )
 
     loop(0, 15, send_row)
-    xall[0, pl.ds(own_slot, 32)] = nrm[c]
+    xall[0, slot_rows(zl, jnp.int32(0))] = nrm[c]
 
     def share(col):
-        rows = pl.ds(pl.multiple_of((rem(col, 2) * 8 + div(col, 2)) * 32, 32), 32)
+        rows = slot_rows(rem(col, 2), rem(y - div(col, 2) + 8, 8))
         piece = xall.at[0, rows]
         for d in (2, 1, 3):
             dev = (x_row(rem(x + d, 4)), c)
@@ -223,30 +230,30 @@
         share(rem(c - k + 16, 16))
 
     share(c)
-    loop(0, EARLY, pass_row)
-
-    arrived(b1buf.at[pl.ds(0, 7)], b1_r)
     lane_group = lax.broadcasted_iota(jnp.int32, (16, 128), 1) // 32
-    for g in range(2):
-        tiles = [b1buf[4 * g + i].astype(jnp.float32) for i in range(4)]
+
+    def spread_bias(half, first, count):
+        loop(first, first + count, lambda n: arrived(b1buf.at[0], b1_r.at[n]))
+        tiles = [b1buf[4 * half + i].astype(jnp.float32) for i in range(4)]
         for h in range(4):
             merged = jnp.zeros((16, 128), jnp.float32)
             for i in range(4):
                 turn = (i - h) * 32 % 128
                 moved = pltpu.roll(tiles[i], turn, 1) if turn else tiles[i]
                 merged = jnp.where(lane_group == i, moved, merged)
-            bbuf[core, z, h * 16 : (h + 1) * 16, g * 128 : (g + 1) * 128] = merged.astype(
-                jnp.bfloat16
-            )
-    own_bias = bbuf.at[core, z]
-
-    def send_bias(n):
-        k = outward(n, 4)
-        send(own_bias, own_bias, b2_s.at[k], b2_r.at[k], z_peer(k))
-
-    loop(0, 7, send_bias)
-    send(own_bias, own_bias, b3_s.at[0], b3_r.at[0], sibling)
-
+            bbuf[core, z, half, h * 16 : (h + 1) * 16] = merged.astype(jnp.bfloat16)
+        block = bbuf.at[core, z, half]
+
+        def send_bias(n):
+            k = outward(n, 4)
+            send(block, block, b2_s, b2_r.at[half * 8 + k], z_peer(k))
+
+        loop(0, 7, send_bias)
+        send(block, block, b3_s, b3_r.at[half * 8], sibling)
+
+    spread_bias(1, 4, 3)
+    loop(0, EARLY, pass_row)
+    spread_bias(0, 0, 4)
     loop(EARLY, 15, pass_row)
     loads[3].wait()
     wkt[...] = wk_ref[...].astype(jnp.float32).T.astype(jnp.bfloat16)
@@ -260,8 +267,8 @@
                 head_of_key == h, values, 0.0
             ).astype(jnp.bfloat16)
         for q in range(4):
-            slot = pl.multiple_of(((q % 2) * 8 + 2 * x + q // 2) * 32, 32)
-            xq[q * 32 : (q + 1) * 32] = xall[d, pl.ds(slot, 32)]
+            k = rem(y - 2 * x - q // 2 + 8, 8)
+            xq[q * 32 : (q + 1) * 32] = xall[d, slot_rows(q % 2, k)]
         own = xq[...]
         gbuf[d] = jax.nn.sigmoid(dot(own, wg_ref[...]))
         queries = (dot(own, wq_ref[...]) * 32**-0.5).astype(jnp.bfloat16)
@@ -272,11 +279,12 @@
         ]
         scores[d] = dot(jnp.concatenate(by_head, 0), kt)
 
-    def lay_bias(half, zz):
-        block = bbuf[half, zz].astype(jnp.float32)
-        j0 = pl.multiple_of((div(zz, 2) * 2 + half) * 16, 16)
+    def lay_bias(side, zz, half):
+        block = bbuf[side, zz, half].astype(jnp.float32)
+        j0 = pl.multiple_of((div(zz, 2) * 2 + side) * 16, 16)
+        lanes = slice(half * 128, half * 128 + 128)
         for h in range(4):
-            biasf[rem(zz, 2), h, pl.ds(j0, 16)] = block[h * 16 : (h + 1) * 16]
+            biasf[rem(zz, 2), h, pl.ds(j0, 16), lanes] = block[h * 16 : (h + 1) * 16]
 
     head_of_lane = lax.broadcasted_iota(jnp.int32, (128, 128), 1) // 32
     head_of_key = lax.broadcasted_iota(jnp.int32, (512, 128), 1) // 32
@@ -284,33 +292,40 @@
     for load in loads[4:]:
         load.wait()
     project(0)
-    lay_bias(core, z)
-
-    def forward(n):
-        k = outward(6 - n, 4)
-        zz = rem(z - k + 8, 8)
-        block = bbuf.at[core, zz]
-        arrived(block, b2_r.at[k])
-        send(block, block, b3_s.at[k], b3_r.at[k], sibling)
-        lay_bias(core, zz)
-
-    loop(0, 7, forward)
+    lay_bias(core, z, 0)
+    lay_bias(core, z, 1)
+
+    def forward(half):
+        def one(n):
+            k = outward(6 - n, 4)
+            zz = rem(z - k + 8, 8)
+            block = bbuf.at[core, zz, half]
+            arrived(block, b2_r.at[half * 8 + k])
+            send(block, block, b3_s, b3_r.at[half * 8 + k], sibling)
+            lay_bias(core, zz, half)
+
+        loop(0, 7, one)
 
     def next_row(d):
         arrived(xall.at[d], s2_r.at[d])
         project(d)
 
+    def take_bias(half):
+        def one(n):
+            k = outward(7 - n, 4)
+            zz = rem(z - k + 8, 8)
+            arrived(bbuf.at[0, 0, 0], b3_r.at[half * 8 + k])
+            lay_bias(1 - core, zz, half)
+
+        loop(0, 8, one)
+
+    forward(1)
     next_row(1)
     next_row(3)
+    forward(0)
     next_row(2)
-
-    def take_bias(n):
-        k = outward(7 - n, 4)
-        zz = rem(z - k + 8, 8)
-        arrived(bbuf.at[0, 0], b3_r.at[k])
-        lay_bias(1 - core, zz)
-
-    loop(0, 8, take_bias)
+    take_bias(1)
+    take_bias(0)
 
     def weigh(d):
         scale = jnp.zeros((128, 128), jnp.float32)
@@ -337,38 +352,16 @@
         here = jnp.logical_and(to_row == r, to_col == c)
         return src, dst, (to_row, to_col), here
 
-    def emit(d):
-        if d > 0:
-            dev = (x_row(rem(x - d + 4, 4)), c)
-            send(ustage.at[d], ufull.at[x], o1_s.at[d], o1_r.at[d], dev)
-
-        def one(n):
-            t = rem(zh * 2 + 4 + n, 8)
-            src, dst, dev, here = mirror_copy(d, t)
-
-            @pl.when(here)
-            def _():
-                pltpu.make_async_copy(src, dst, m_r).start()
-
-            @pl.when(jnp.logical_not(here))
-            def _():
-                send(src, dst, m_s, m_r, dev)
-
-        loop(0, 8, one)
-
-    weigh(2)
-    weigh(1)
-    mix(2)
-    emit(2)
-    weigh(3)
-    mix(1)
-    emit(1)
-    weigh(0)
-    mix(3)
-    emit(3)
-    mix(0)
-    emit(0)
-    ufull[x] = ustage[0]
+    def mirror_row(d, t):
+        src, dst, dev, here = mirror_copy(d, t)
+
+        @pl.when(here)
+        def _():
+            pltpu.make_async_copy(src, dst, m_r).start()
+
+        @pl.when(jnp.logical_not(here))
+        def _():
+            send(src, dst, m_s, m_r, dev)
 
     def give(group):
         def one(q):
@@ -386,7 +379,37 @@
 
         loop(0, 4, one)
 
-    give(x)
+    def emit(d):
+        @pl.when(d > 0)
+        def _():
+            dev = (x_row(rem(x - d + 4, 4)), c)
+            send(ustage.at[d], ufull.at[x], o1_s.at[d], o1_r.at[d], dev)
+
+        loop(0, 4, lambda t: mirror_row(d, t))
+
+        @pl.when(d == 0)
+        def _():
+            ufull[x] = ustage[0]
+            give(x)
+
+    far = rem(div(rem(y - div(zh, 2) + 8, 8) + 4, 2), 4)
+    high = div(zh, 2)
+    order = [
+        d + high * (rem(x - rem(far + step, 4) + 4, 4) - d)
+        for d, step in ((2, 0), (1, 1), (3, 3), (0, 2))
+    ]
+    weigh(order[0])
+    weigh(order[1])
+    mix(order[0])
+    emit(order[0])
+    weigh(order[2])
+    mix(order[1])
+    emit(order[1])
+    weigh(order[3])
+    mix(order[2])
+    emit(order[2])
+    mix(order[3])
+    emit(order[3])
 
     def pass_on(d):
         arrived(ufull.at[0], o1_r.at[d])
@@ -395,11 +418,13 @@
     pass_on(2)
     pass_on(1)
     pass_on(3)
+    for d in order:
+        loop(4, 8, lambda t: mirror_row(d, t))
 
     arrived(b1buf.at[pl.ds(0, 7)], b1_s)
     arrived(nrm.at[pl.ds(0, 15)], s1_s)
-    loop(1, 8, lambda k: arrived(bbuf.at[0, 0], b2_s.at[k]))
-    loop(0, 8, lambda k: arrived(bbuf.at[0, 0], b3_s.at[k]))
+    arrived(bbuf.at[0, pl.ds(0, 7)], b2_s)
+    arrived(bbuf.at[0], b3_s)
     loop(1, 4, lambda d: arrived(xall.at[0], s2_s.at[d]))
     loop(1, 4, lambda d: arrived(ustage.at[0], o1_s.at[d]))
 
@@ -463,7 +488,7 @@
             pltpu.VMEM((128, 2048), bf16),
             pltpu.VMEM((64, 2048), bf16),
             pltpu.VMEM((8, 16, 128), bf16),
-            pltpu.VMEM((2, 8, 64, 256), bf16),
+            pltpu.VMEM((2, 8, 2, 64, 128), bf16),
             pltpu.VMEM((2, 4, 128, 256), f32),
             pltpu.VMEM((4, 512, 128), bf16),
             pltpu.VMEM((128, 128), bf16),
@@ -482,11 +507,11 @@
             dma((4,)),
             dma((4,)),
             dma,
-            dma,
             dma((8,)),
-            dma((8,)),
-            dma((8,)),
-            dma((8,)),
+            dma,
+            dma((16,)),
+            dma,
+            dma((16,)),
             dma((4,)),
             dma((4,)),
             dma,

time: 43.3 us -> 41.5 us (0.958)
  Pallas kernels: 42.4 us -> 40.5 us
    pallas_call x1, Pallas kernels: 41.7 us -> 39.8 us  [per_device(): pl.pallas_call(kernel, out_shape=(near, near), in_specs=[hbm] * 8, out_sp...]
where the time goes in v5:
time: 41.5 us; the launch traced here: 41.1 us
  Pallas kernels  40.5 us (98%)
  between operations  0.64 us (2%)
    pallas_call x1, Pallas kernels, per_device(): pl.pallas_call(kernel, out_shape=(near, near), in_specs=[hbm] * 8, out_sp...  39.8 us

profile of v5, /device:TPU:1, one launch (start us, length us, event | category | flops | bytes accessed | tf_op | source)
XLA Modules:
  0.0 41.1 jit_solution(8313814605811170980)
XLA Ops:
  0.6 39.8 %shard_map.95 = (bf16[16,32,128]{2,1,0:T(8,128)(2,1)S(1)}, bf16[16,32,128]{2,1,0:T(8,128)(2,1)S(1)}) custom-call(bf16[16,32,128]{2,1,0:T(8,128)(2,1)} %pair_hbm.1, bf16[1,128]{1,0:T(2,128)(2,1)} %bitcast.3, bf16[128,128]{1,0:T(8,128)(2,1)} %wq_hbm.1, bf16[128,128]{1,0:T(8,128)(2,1)} %wk_hbm.1, bf16[128,128]{1,0:T(8,128)(2,1)} %wv_hbm.1, ...), custom_call_target="tpu_custom_call" | custom-call | flops 1000000000 | bytes 1000000 | tf_op jit(solution)/shard_map/pallas_call | solution.py:472
  40.4 0.7 %shard_map.96 = (bf16[16,32,128]{2,1,0:T(8,128)(2,1)}, bf16[16,32,128]{2,1,0:T(8,128)(2,1)}) custom-call(bf16[16,32,128]{2,1,0:T(8,128)(2,1)S(1)} %get-tuple-element.4.upd, bf16[16,32,128]{2,1,0:T(8,128)(2,1)S(1)} %get-tuple-element.5.mir), custom_call_target="tpu_custom_call" | custom-call | bytes 524288 | tf_op jit(solution)/shard_map/pallas_call | solution.py:529

commit v6 on v5

--- a/solution.py
+++ b/solution.py
@@ -291,9 +291,6 @@
 
     for load in loads[4:]:
         load.wait()
-    project(0)
-    lay_bias(core, z, 0)
-    lay_bias(core, z, 1)
 
     def forward(half):
         def one(n):
@@ -302,9 +299,9 @@
             block = bbuf.at[core, zz, half]
             arrived(block, b2_r.at[half * 8 + k])
             send(block, block, b3_s, b3_r.at[half * 8 + k], sibling)
-            lay_bias(core, zz, half)
 
         loop(0, 7, one)
+        loop(1, 8, lambda k: lay_bias(core, rem(z + k, 8), half))
 
     def next_row(d):
         arrived(xall.at[d], s2_r.at[d])
@@ -320,9 +317,12 @@
         loop(0, 8, one)
 
     forward(1)
+    lay_bias(core, z, 0)
+    lay_bias(core, z, 1)
+    project(0)
+    forward(0)
     next_row(1)
     next_row(3)
-    forward(0)
     next_row(2)
     take_bias(1)
     take_bias(0)

time: 41.5 us -> 41.1 us (level)
  the two profiles are of different devices: /device:TPU:1 before, /device:TPU:16 now
where the time goes in v6:
time: 41.1 us; the launch traced here: 41 us
  Pallas kernels  40.3 us (98%)
  between operations  0.64 us (2%)
    pallas_call x1, Pallas kernels, per_device(): pl.pallas_call(kernel, out_shape=(near, near), in_specs=[hbm] * 8, out_sp...  39.6 us

profile of v6, /device:TPU:16, one launch (start us, length us, event | category | flops | bytes accessed | tf_op | source)
XLA Modules:
  0.0 41.0 jit_solution(8031058332826855960)
XLA Ops:
  0.6 39.6 %shard_map.95 = (bf16[16,32,128]{2,1,0:T(8,128)(2,1)S(1)}, bf16[16,32,128]{2,1,0:T(8,128)(2,1)S(1)}) custom-call(bf16[16,32,128]{2,1,0:T(8,128)(2,1)} %pair_hbm.1, bf16[1,128]{1,0:T(2,128)(2,1)} %bitcast.3, bf16[128,128]{1,0:T(8,128)(2,1)} %wq_hbm.1, bf16[128,128]{1,0:T(8,128)(2,1)} %wk_hbm.1, bf16[128,128]{1,0:T(8,128)(2,1)} %wv_hbm.1, ...), custom_call_target="tpu_custom_call" | custom-call | flops 1000000000 | bytes 1000000 | tf_op jit(solution)/shard_map/pallas_call | solution.py:472
  40.3 0.7 %shard_map.96 = (bf16[16,32,128]{2,1,0:T(8,128)(2,1)}, bf16[16,32,128]{2,1,0:T(8,128)(2,1)}) custom-call(bf16[16,32,128]{2,1,0:T(8,128)(2,1)S(1)} %get-tuple-element.4.upd, bf16[16,32,128]{2,1,0:T(8,128)(2,1)S(1)} %get-tuple-element.5.mir), custom_call_target="tpu_custom_call" | custom-call | bytes 524288 | tf_op jit(solution)/shard_map/pallas_call | solution.py:529

commit v7 on v6

--- a/solution.py
+++ b/solution.py
@@ -204,7 +204,7 @@
         return pl.ds(pl.multiple_of((z_low * 8 + position(k)) * 32, 32), 32)
 
     def send_row(n):
-        k = outward(n, 8)
+        k = outward(14 - n, 8)
         col = rem(c + k, 16)
         send(
             nrm.at[col],
@@ -399,9 +399,9 @@
         for d, step in ((2, 0), (1, 1), (3, 3), (0, 2))
     ]
     weigh(order[0])
-    weigh(order[1])
     mix(order[0])
     emit(order[0])
+    weigh(order[1])
     weigh(order[2])
     mix(order[1])
     emit(order[1])

time: 41.1 us -> 40.5 us (0.985)
  the two profiles are of different devices: /device:TPU:16 before, /device:TPU:6 now
where the time goes in v7:
time: 40.5 us; the launch traced here: 40.4 us
  Pallas kernels  39.7 us (98%)
  between operations  0.64 us (2%)
    pallas_call x1, Pallas kernels, per_device(): pl.pallas_call(kernel, out_shape=(near, near), in_specs=[hbm] * 8, out_sp...  39 us

profile of v7, /device:TPU:6, one launch (start us, length us, event | category | flops | bytes accessed | tf_op | source)
XLA Modules:
  0.0 40.4 jit_solution(82368577145758356)
XLA Ops:
  0.6 39.0 %shard_map.95 = (bf16[16,32,128]{2,1,0:T(8,128)(2,1)S(1)}, bf16[16,32,128]{2,1,0:T(8,128)(2,1)S(1)}) custom-call(bf16[16,32,128]{2,1,0:T(8,128)(2,1)} %pair_hbm.1, bf16[1,128]{1,0:T(2,128)(2,1)} %bitcast.3, bf16[128,128]{1,0:T(8,128)(2,1)} %wq_hbm.1, bf16[128,128]{1,0:T(8,128)(2,1)} %wk_hbm.1, bf16[128,128]{1,0:T(8,128)(2,1)} %wv_hbm.1, ...), custom_call_target="tpu_custom_call" | custom-call | flops 1000000000 | bytes 1000000 | tf_op jit(solution)/shard_map/pallas_call | solution.py:472
  39.6 0.7 %shard_map.96 = (bf16[16,32,128]{2,1,0:T(8,128)(2,1)}, bf16[16,32,128]{2,1,0:T(8,128)(2,1)}) custom-call(bf16[16,32,128]{2,1,0:T(8,128)(2,1)S(1)} %get-tuple-element.4.upd, bf16[16,32,128]{2,1,0:T(8,128)(2,1)S(1)} %get-tuple-element.5.mir), custom_call_target="tpu_custom_call" | custom-call | bytes 524288 | tf_op jit(solution)/shard_map/pallas_call | solution.py:529

commit v8 on v7

--- a/solution.py
+++ b/solution.py
@@ -398,18 +398,10 @@
         d + high * (rem(x - rem(far + step, 4) + 4, 4) - d)
         for d, step in ((2, 0), (1, 1), (3, 3), (0, 2))
     ]
-    weigh(order[0])
-    mix(order[0])
-    emit(order[0])
-    weigh(order[1])
-    weigh(order[2])
-    mix(order[1])
-    emit(order[1])
-    weigh(order[3])
-    mix(order[2])
-    emit(order[2])
-    mix(order[3])
-    emit(order[3])
+    for d in order:
+        weigh(d)
+        mix(d)
+        emit(d)
 
     def pass_on(d):
         arrived(ufull.at[0], o1_r.at[d])

time: 40.5 us -> 40.2 us (level)
  no operation moved by 1% of the time
where the time goes in v8:
time: 40.2 us; the launch traced here: 40.1 us
  Pallas kernels  39.4 us (98%)
  between operations  0.64 us (2%)
    pallas_call x1, Pallas kernels, per_device(): pl.pallas_call(kernel, out_shape=(near, near), in_specs=[hbm] * 8, out_sp...  38.7 us

profile of v8, /device:TPU:6, one launch (start us, length us, event | category | flops | bytes accessed | tf_op | source)
XLA Modules:
  0.0 40.1 jit_solution(3939064517634345247)
XLA Ops:
  0.6 38.7 %shard_map.95 = (bf16[16,32,128]{2,1,0:T(8,128)(2,1)S(1)}, bf16[16,32,128]{2,1,0:T(8,128)(2,1)S(1)}) custom-call(bf16[16,32,128]{2,1,0:T(8,128)(2,1)} %pair_hbm.1, bf16[1,128]{1,0:T(2,128)(2,1)} %bitcast.3, bf16[128,128]{1,0:T(8,128)(2,1)} %wq_hbm.1, bf16[128,128]{1,0:T(8,128)(2,1)} %wk_hbm.1, bf16[128,128]{1,0:T(8,128)(2,1)} %wv_hbm.1, ...), custom_call_target="tpu_custom_call" | custom-call | flops 1000000000 | bytes 1000000 | tf_op jit(solution)/shard_map/pallas_call | solution.py:464
  39.4 0.7 %shard_map.96 = (bf16[16,32,128]{2,1,0:T(8,128)(2,1)}, bf16[16,32,128]{2,1,0:T(8,128)(2,1)}) custom-call(bf16[16,32,128]{2,1,0:T(8,128)(2,1)S(1)} %get-tuple-element.4.upd, bf16[16,32,128]{2,1,0:T(8,128)(2,1)S(1)} %get-tuple-element.5.mir), custom_call_target="tpu_custom_call" | custom-call | bytes 524288 | tf_op jit(solution)/shard_map/pallas_call | solution.py:521
